TPU v7x, 128 devices: a whole 4x4x4 slice. The times are simulated.
128 devices in a mesh: energy: 16 (over z, y), slab: 8 (over x, core).
Axes of the slice: x: 4, y: 4, z: 4, core: 2. Of those that a mesh axis runs over, the one named last changes fastest.
Arguments:
- occupancy: int32 [16, 256], P('slab', 'energy'), may hold values from 0 to 2
- onsite: float32 [16, 256], P('slab', 'energy'), may hold values from 0 to 1
- defect_shift: float32 [16, 256], P('slab', 'energy'), may hold values from 0.3 to 1.5
- site_order: int32 [256], replicated, may hold values from 0 to 255, each once
- lateral: float32 [16, 256, 256], P('slab', 'energy'), may hold values from -4.5 to 4.5
- coupling: float32 [16, 256], P('slab'), may hold values from 2 to 3
- energies: float32 [16], P('energy'), may hold values from 1.5 to 3.5
- weights: float32 [16], P('energy'), may hold values from 0.05 to 0.25
- sources: float32 [2, 16, 16, 256], P(None, 'energy', 'slab'), may hold values from -6 to 6
Outputs:
- site_density: float32 [16, 256], P('slab', 'energy')
Inputs may be any that keep to these rules, and one draw needn't show every extreme that they name: `site_order`: a permutation of the 256 orbitals of a block.
All inputs are finite; a program needn't handle non-finite values.
Results may differ from a plain program's by a relative error of at most 0.0003.
Values sent between devices are 32-bit elements; how exact they have to be, the bound alone decides.
No kernel may reach another device: no remote copies, remote signals or barrier semaphores. Data moves between devices by JAX's collectives and lax.ppermute only.
A program may use at most 128 MiB of HBM per device.

v0:
```python
import jax
import jax.numpy as jnp
from jax import lax
from jax.sharding import PartitionSpec as P

BROADENING = 1.2
LATERAL_SCALE = 0.9
HIGHEST = lax.Precision.HIGHEST
BASE_WIDTH = 64


def shifted(array, axis, by):
    size = lax.axis_size(axis)
    pairs = [(i, i + by) for i in range(size) if 0 <= i + by < size]
    return lax.ppermute(array, axis, pairs)


def real_product(first_mat, second_mat):
    return jnp.einsum(
        "ekl,elm->ekm", first_mat, second_mat, precision=HIGHEST, preferred_element_type=jnp.float32
    )


def mat_mul(first_mat, second_mat):
    real_part = real_product(first_mat[0], second_mat[0]) - real_product(
        first_mat[1], second_mat[1]
    )
    imag_part = real_product(first_mat[0], second_mat[1]) + real_product(
        first_mat[1], second_mat[0]
    )
    return jnp.stack([real_part, imag_part])


def real_apply(matrix, vector):
    return jnp.einsum(
        "ekl,el->ek", matrix, vector, precision=HIGHEST, preferred_element_type=jnp.float32
    )


def mat_vec(matrix, vector):
    real_part = real_apply(matrix[0], vector[0]) - real_apply(matrix[1], vector[1])
    imag_part = real_apply(matrix[0], vector[1]) + real_apply(matrix[1], vector[0])
    return jnp.stack([real_part, imag_part])


def invert_direct(matrix):
    width = matrix.shape[-1]
    upper_half = jnp.concatenate([matrix[0], -matrix[1]], axis=2)
    lower_half = jnp.concatenate([matrix[1], matrix[0]], axis=2)
    system = jnp.concatenate([upper_half, lower_half], axis=1)
    normal = jnp.einsum(
        "eji,ejk->eik", system, system, precision=HIGHEST, preferred_element_type=jnp.float32
    )
    factor = jnp.linalg.cholesky(normal)
    answer = jax.scipy.linalg.cho_solve((factor, True), jnp.swapaxes(system, 1, 2))
    unit_matrix = jnp.eye(2 * width, dtype=jnp.float32)
    leftover = unit_matrix[None] - jnp.einsum(
        "eij,ejk->eik", system, answer, precision=HIGHEST, preferred_element_type=jnp.float32
    )
    answer = answer + jnp.einsum(
        "eij,ejk->eik", answer, leftover, precision=HIGHEST, preferred_element_type=jnp.float32
    )
    return jnp.stack([answer[:, :width, :width], answer[:, width:, :width]])


def invert(matrix):
    width = matrix.shape[-1]
    if width <= BASE_WIDTH or width % 2 != 0:
        return invert_direct(matrix)
    half = width // 2
    top_left = matrix[:, :, :half, :half]
    top_right = matrix[:, :, :half, half:]
    bottom_left = matrix[:, :, half:, :half]
    bottom_right = matrix[:, :, half:, half:]
    first_inverse = invert(top_left)
    left_times = mat_mul(first_inverse, top_right)
    lower_times = mat_mul(bottom_left, first_inverse)
    schur_inverse = invert(bottom_right - mat_mul(bottom_left, left_times))
    new_top_right = -mat_mul(left_times, schur_inverse)
    new_bottom_left = -mat_mul(schur_inverse, lower_times)
    new_top_left = first_inverse - mat_mul(new_top_right, lower_times)
    upper_rows = jnp.concatenate([new_top_left, new_top_right], axis=3)
    lower_rows = jnp.concatenate([new_bottom_left, schur_inverse], axis=3)
    return jnp.concatenate([upper_rows, lower_rows], axis=2)


def scale_rows(bond, matrix):
    return matrix * bond[:, None]


def block_matrix(energies, pot_row, hop_block, identity):
    real_part = (energies[:, None] - pot_row[None, :])[:, :, None] * identity - hop_block[None]
    imag_part = jnp.broadcast_to(BROADENING * identity, real_part.shape)
    return jnp.stack([real_part, imag_part])


def shards(
    occupancy, onsite, defect_shift, site_order, lateral, coupling, energies, weights, sources
):
    pot_piece = onsite + occupancy.astype(jnp.float32) * defect_shift
    lateral_rows, brick_pot = (
        lax.all_gather(lateral, "energy", axis=1, tiled=True),
        lax.all_gather(pot_piece, "energy", axis=1, tiled=True),
    )
    potential = jnp.zeros_like(brick_pot).at[:, site_order].set(brick_pot)
    hopping = LATERAL_SCALE * (lateral_rows + jnp.swapaxes(lateral_rows, 1, 2))
    identity = jnp.eye(coupling.shape[1], dtype=jnp.float32)
    block_count = coupling.shape[0]
    inner_count = block_count - 1
    prev_bond = shifted(coupling[block_count - 1], "slab", 1)
    block = 0
    matrix = block_matrix(energies, potential[block], hopping[block], identity)
    source_now = sources[:, :, block]
    inverse = invert(matrix)
    left_link = inverse * prev_bond
    part = mat_vec(inverse, source_now)
    links = [inverse * coupling[block]]
    lefts = [left_link]
    parts = [part]
    first_right = links[inner_count - 1]
    first_left = lefts[inner_count - 1]
    first_part = parts[inner_count - 1]
    next_right, next_left, next_part = shifted((first_right, first_left, first_part), "slab", -1)
    bond_pen = coupling[block_count - 2]
    bond_last = coupling[block_count - 1]
    last_matrix = block_matrix(
        energies, potential[block_count - 1], hopping[block_count - 1], identity
    )
    reduced_diag = (
        last_matrix
        - scale_rows(bond_pen, links[inner_count - 1])
        - scale_rows(bond_last, next_left)
    )
    lower = scale_rows(bond_pen, lefts[inner_count - 1])
    upper = scale_rows(bond_last, next_right)
    rhs = sources[:, :, block_count - 1] + bond_pen * parts[inner_count - 1] + bond_last * next_part
    all_diag, all_lower, all_upper, all_rhs = (
        lax.all_gather(reduced_diag[None], "slab", axis=0, tiled=True),
        lax.all_gather(lower[None], "slab", axis=0, tiled=True),
        lax.all_gather(upper[None], "slab", axis=0, tiled=True),
        lax.all_gather(rhs[None], "slab", axis=0, tiled=True),
    )

    def forward(state_pair, items):
        prev_link, prev_part = state_pair
        block_diag, block_lower, block_upper, block_rhs = items
        schur = block_diag - mat_mul(block_lower, prev_link)
        inverse = invert(schur)
        link = mat_mul(inverse, block_upper)
        part = mat_vec(inverse, block_rhs + mat_vec(block_lower, prev_part))
        return ((link, part), (link, part))

    _, (chain_links, chain_parts) = lax.scan(
        forward,
        (jnp.zeros_like(reduced_diag), jnp.zeros_like(rhs)),
        (all_diag, all_lower, all_upper, all_rhs),
    )

    def backward(later, items):
        link, part = items
        value = part + mat_vec(link, later)
        return (value, value)

    _, solved = lax.scan(backward, jnp.zeros_like(rhs), (chain_links, chain_parts), reverse=True)
    odd_psi = lax.dynamic_index_in_dim(solved, lax.axis_index("slab"), 0, keepdims=False)
    prev_odd = shifted(odd_psi, "slab", 1)
    solved_blocks = [odd_psi]
    later = odd_psi
    block = 0
    later = mat_vec(links[block], later) + mat_vec(lefts[block], prev_odd) + parts[block]
    solved_blocks.append(later)
    psi_blocks = jnp.stack(solved_blocks[::-1], axis=2)
    local_density = jnp.einsum(
        "e,cejk->jk",
        weights,
        psi_blocks * psi_blocks,
        precision=HIGHEST,
        preferred_element_type=jnp.float32,
    )
    return lax.psum_scatter(local_density, "energy", scatter_dimension=1, tiled=True)


def solution(mesh):
    return jax.shard_map(
        shards,
        mesh=mesh,
        in_specs=(
            P("slab", "energy"),
            P("slab", "energy"),
            P("slab", "energy"),
            P(),
            P("slab", "energy", None),
            P("slab", None),
            P("energy"),
            P("energy"),
            P(None, "energy", "slab", None),
        ),
        out_specs=P("slab", "energy"),
        check_vma=False,
    )
```

profile of v0, /device:TPU:1, one launch (start us, length us, event | category | flops | bytes accessed | tf_op | source)
XLA Modules:
  0.0 1423.6 jit_solution(1403582596609567399)
XLA Ops:
  12.6 21.3 %all_gather.19 = f32[2,256,256]{2,0,1:T(2,128)S(1)} all-gather(f32[2,16,256]{2,0,1:T(2,128)S(1)} %copy.134), channel_id=1, replica_groups=mesh['energy'=16,'slab'=8] {'energy'}, dimensions={1}, use_global_device_ids=true | all-gather | bytes 557056 | tf_op jit(solution)/shard_map/all_gather | solution.py:102
  35.0 16.2 %all-gather.3 = f32[16,16,2]{1,2,0:T(2,128)S(1)} all-gather(f32[1,16,2]{1,2,0:T(2,128)S(1)} %add_bitcast_fusion), channel_id=1, replica_groups=mesh['energy'=16,'slab'=8] {'energy'}, dimensions={0}, use_global_device_ids=true | all-gather | bytes 2176 | tf_op jit(solution)/shard_map/all_gather | solution.py:103
  54.7 11.7 custom-call.31
  80.9 11.7 custom-call.33
  93.9 10.0 custom-call.34
  110.0 11.7 custom-call.35
  136.4 11.7 custom-call.37
  167.9 11.5 collective-permute-start.2
  187.6 16.6 %collective-permute-done.1 = f32[2,1,256,256]{3,2,0,1:T(8,128)S(1)} collective-permute-done((f32[2,1,256,256]{3,2,0,1:T(8,128)S(1)}, f32[2,1,256,256]{3,2,0,1:T(8,128)S(1)}, u32[]{:S(2)}, u32[]{:S(2)}) %collective-permute-start.1) | collective-permute-done | bytes 524320 | tf_op jit(solution)/shard_map/ppermute | solution.py:15
  212.4 10.9 all-gather.2
  223.3 20.5 %all-gather.10.cloned.1.call-done = f32[16,1,256,256]{3,2,1,0:T(8,128)} async-done(((f32[2,1,256,256]{3,2,1,0:T(8,128)}), f32[16,1,256,256]{3,2,1,0:T(8,128)}) %all-gather.10.cloned.1.call-update) | async-done | bytes 4194320 | tf_op jit(solution)/shard_map/all_gather | solution.py:138
  243.8 33.8 %all-gather.12.cloned.1.call-done = f32[16,1,256,256]{3,2,1,0:T(8,128)} async-done(((f32[2,1,256,256]{3,2,1,0:T(8,128)}), f32[16,1,256,256]{3,2,1,0:T(8,128)}) %all-gather.12.cloned.1.call-update) | async-done | bytes 4194320 | tf_op jit(solution)/shard_map/all_gather | solution.py:140
  277.7 1058.1 %while.33 = (s32[]{:T(128)}, f32[2,1,256,256]{3,2,1,0:T(8,128)S(1)}, f32[2,1,256]{2,1,0:T(1,128)S(1)}, f32[8,2,1,256,256]{4,3,1,2,0:T(8,128)}, f32[8,2,1,256]{3,...) while((s32[]{:T(128)}, ...), condition=%wide.region_4.7_spmd, body=%wide.region_3.6_spmd.sunk | while | flops 2879196160 | bytes 32623276 | solution.py:153
  285.1 11.7 custom-call.48
  298.1 9.8 custom-call.49
  311.5 11.9 custom-call.50
  340.2 11.7 custom-call.52
  366.7 11.7 custom-call.54
  416.9 11.7 custom-call.48
  443.3 12.1 custom-call.50
  472.3 11.7 custom-call.52
  498.5 11.7 custom-call.54
  549.0 11.7 custom-call.48
  575.4 11.9 custom-call.50
  604.1 11.7 custom-call.52
  630.6 11.7 custom-call.54
  680.8 11.7 custom-call.48
  707.2 12.1 custom-call.50
  736.1 11.7 custom-call.52
  762.4 11.7 custom-call.54
  812.8 11.7 custom-call.48
  839.2 11.9 custom-call.50
  867.9 11.7 custom-call.52
  894.4 11.7 custom-call.54
  944.6 11.7 custom-call.48
  971.0 12.1 custom-call.50
  999.9 11.7 custom-call.52
  1026.2 11.7 custom-call.54
  1076.6 11.7 custom-call.48
  1103.0 11.9 custom-call.50
  1131.7 11.7 custom-call.52
  1158.2 11.7 custom-call.54
  1208.4 11.7 custom-call.48
  1234.8 12.1 custom-call.50
  1263.8 11.7 custom-call.52
  1290.0 11.7 custom-call.54
  1335.8 41.6 %while.34 = (s32[]{:T(128)}, f32[2,1,256]{2,1,0:T(1,128)S(1)}, f32[8,2,1,256]{3,2,1,0:T(1,128)S(1)}, f32[8,2,1,256]{3,2,1,0:T(1,128)S(1)}, f32[8,2,1,256,256]{4,...) while((s32[]{:T(128)}, f32[2,1,256]{2,1,0:T(1,128)S(1)}, ...), condition=%wide.region_6.9_spmd.clone, body=%wide.region_5.8_spmd.clone.sunk | while | flops 3148805 | bytes 1079455 | solution.py:164
  1382.8 33.4 %all-reduce = f32[2,256]{1,0:T(2,128)S(1)} all-reduce(f32[2,256]{1,0:T(2,128)S(1)} %broadcast_multiply_fusion.2), channel_id=5, replica_groups=mesh['energy'=16,'slab'=8] {'energy'}, use_global_device_ids=true, to_apply=%region_8.11.clone | all-reduce | flops 512 | bytes 4096
  (1609 shorter events, 783.4 us)
Async XLA Ops:
  6.5 216.8 %all-gather.8.cloned.1.call-start = ((), (), s32[]{:S(2)}) async-start(), calls=%async_computation | async-start | bytes 4718592 | tf_op jit(solution)/shard_map/all_gather | solution.py:139
  7.3 159.5 %collective-permute-start = (f32[256]{0:T(256)S(1)}, f32[256]{0:T(256)S(1)}, u32[]{:S(2)}, u32[]{:S(2)}) collective-permute-start(f32[256]{0:T(256)S(1)} %bitcast.1805), channel_id=1, source_target_pairs={{0,1},{1,2},{2,3},{3,4},{4,5},{5,6},{6,7},{8,9},{9,10},{10,11},{11... | collective-permute-start | bytes 3080 | tf_op jit(solution)/shard_map/ppermute | solution.py:15
  166.8 39.3 %copy-start = (f32[2,1,2,256]{3,2,1,0:T(2,128)S(1)}, f32[2,1,2,256]{3,2,1,0:T(2,128)}, u32[]{:S(2)}) copy-start(f32[2,1,2,256]{3,2,1,0:T(2,128)} %param.24) | copy-start | bytes 12292
  167.7 42.3 %copy-start.1 = (u32[128]{0:T(128)S(1)}, u32[128]{0:T(128)}, u32[]{:S(2)}) copy-start(u32[128]{0:T(128)} %constant.126) | copy-start | bytes 1540
  167.8 76.1 %all-gather.10.cloned.1.call-start = ((), (), s32[]{:S(2)}) async-start(), calls=%async_computation.1 | async-start | bytes 4718592 | tf_op jit(solution)/shard_map/all_gather | solution.py:138
  167.9 19.6 %collective-permute-start.2 = (f32[2,1,256,256]{3,2,0,1:T(8,128)S(1)}, f32[2,1,256,256]{3,2,0,1:T(8,128)S(1)}, u32[]{:S(2)}, u32[]{:S(2)}) collective-permute-start(f32[2,1,256,256]{3,2,0,1:T(8,128)S(1)} %get-tuple-element.255), channel_id=1, source_target_pairs={{1,0},{2,1},{3,2},{4,3},{5,4},{6,5},{7,6},{9,8},{10,9},{11,10},{12... | collective-permute-start | bytes 1572872 | tf_op jit(solution)/shard_map/ppermute | solution.py:15
  179.5 24.7 %collective-permute-start.1 = (f32[2,1,256,256]{3,2,0,1:T(8,128)S(1)}, f32[2,1,256,256]{3,2,0,1:T(8,128)S(1)}, u32[]{:S(2)}, u32[]{:S(2)}) collective-permute-start(f32[2,1,256,256]{3,2,0,1:T(8,128)S(1)} %broadcast_multiply_fusion), channel_id=1, source_target_pairs={{1,0},{2,1},{3,2},{4,3},{5,4},{6,5},{7,6},{9,8},{10,9},{11,10},{12... | collective-permute-start | bytes 1572872 | tf_op jit(solution)/shard_map/ppermute | solution.py:15
  205.4 72.2 %all-gather.12.cloned.1.call-start = ((), (), s32[]{:S(2)}) async-start(), calls=%async_computation.2 | async-start | bytes 4718592 | tf_op jit(solution)/shard_map/all_gather | solution.py:140
  207.5 4.9 collective-permute-start.3
  1378.3 3.1 collective-permute-start.4
Sparse Core Ops, SparseCore 0:
  167.9 44.1 all-gather.7
  213.7 30.0 all-gather.9
  245.5 32.0 all-gather.11
where the time goes:
time: 1450 us; the launch traced here: 1420 us
  other arithmetic  850 us (59%)
  matrix products  350 us (24%)
  blocking collectives  81.8 us (6%)
  waiting for transfers between devices  79.3 us (5%)
  starting transfers between devices  22.2 us (2%)
  between operations  16.6 us (1%)
  loops' own time  15.9 us (1%)
    another operation x108, other arithmetic, invert_direct(): factor = jnp.linalg.cholesky(normal)  448 us
    another operation x72, other arithmetic, invert_direct(): jax.scipy.linalg.cho_solve((factor, True), jnp.swapaxes(system, 1, 2))  374 us
    dot_general x712, matrix products, real_product(): jnp.einsum('ekl,elm->ekm', first_mat, second_mat, precision=HIGHEST, pref...  205 us
    dot_general x108, matrix products, real_apply(): jnp.einsum('ekl,el->ek', matrix, vector, precision=HIGHEST, preferred_ele...  93.8 us
    all_gather x1, waiting for transfers between devices, shards(): lax.all_gather(upper[None], 'slab', axis=0, tiled=True)  33.8 us
    unnamed x1, blocking collectives  33.4 us
  transfers between devices with their start and end apart: 8, of which 6 were waited for; matrix products, arithmetic and copies ran while one was open for 8% of the time, Pallas kernels for 0%

commit v1 on v0

v1 whole, which is shorter than its diff:
```python
import functools
import jax
import jax.numpy as jnp
from jax import lax
from jax.experimental import pallas as pl
from jax.experimental.pallas import tpu as pltpu
from jax.sharding import PartitionSpec as P

BROADENING = 1.2
LATERAL_SCALE = 0.9
HIGHEST = lax.Precision.HIGHEST
PACK = 2 * 256 + 8
N=256
W=32
S8=(8,128)
def row(t,s): return jnp.broadcast_to(t[s:s+1],S8)
def lane_of(t,idx): return jnp.take_along_axis(t,idx,axis=1)
def split3(x):
    h=x.astype(jnp.bfloat16); r=x-h.astype(jnp.float32)
    m=r.astype(jnp.bfloat16); l=(r-m.astype(jnp.float32)).astype(jnp.bfloat16)
    return h,m,l
def panel(T,place,sub,lane):
    half=place//128; off=place-128*half
    nt=W//8
    Z=[]
    for s in range(nt):
        pick=lambda t: tuple(jnp.where(half==0,T[t][0][c],T[t][1][c]) for c in (0,1))
        idx=[jnp.full(S8,off+8*s+j,jnp.int32) for j in range(8)]
        src=pick(s)
        C=[(lane_of(src[0],idx[j]),lane_of(src[1],idx[j])) for j in range(8)]
        O={}
        for t in range(s+1,nt):
            o=pick(t)
            O[t]=[(lane_of(o[0],idx[j]),lane_of(o[1],idx[j])) for j in range(8)]
        first=place+8*s
        for h in range(2):
            local=lane-(first-128*h)
            inside=(local>=0)&(local<8)
            minus=jnp.where(local==sub,-1.0,0.0)
            for t in range(s,nt):
                r,i=T[t][h]
                T[t][h]=(jnp.where(inside,minus if t==s else 0.0,r),jnp.where(inside,0.0,i))
        X=[T[s][0],T[s][1]]
        Qr=Qi=None
        rows=[[],[]]
        for j in range(8):
            cr,ci=C[j]
            pr=row(cr,j); pi=row(ci,j)
            inv=1.0/(pr*pr+pi*pi)
            qr=pr*inv; qi=-pi*inv
            Qr=qr if j==0 else jnp.where(sub==j,qr,Qr)
            Qi=qi if j==0 else jnp.where(sub==j,qi,Qi)
            if j<7:
                below=sub>j
                cr=jnp.where(below,cr,0.0); ci=jnp.where(below,ci,0.0)
            def scaled(x,fast=False):
                r=row(x[0],j); i=row(x[1],j)
                if fast: return (r*pr+i*pi)*inv,(i*pr-r*pi)*inv
                return r*qr-i*qi,i*qr+r*qi
            def step(x,w):
                return (x[0]-(cr*w[0]-ci*w[1]),x[1]-(cr*w[1]+ci*w[0]))
            for j2 in range(j+1,8):
                w=scaled(C[j2],j2==j+1)
                C[j2]=step(C[j2],w)
                for t in range(s+1,nt):
                    o,o2=O[t][j],O[t][j2]
                    O[t][j2]=(o2[0]-(o[0]*w[0]-o[1]*w[1]),o2[1]-(o[0]*w[1]+o[1]*w[0]))
            for h in range(2):
                w=scaled(X[h])
                rows[h].append(w)
                if j<7: X[h]=step(X[h],w)
        T[s]=X
        Z.append([(x[0]*Qr-x[1]*Qi,x[1]*Qr+x[0]*Qi) for x in X])
        for t in range(s+1,nt):
            for h in range(2):
                r,i=T[t][h]
                for j in range(8):
                    cr,ci=O[t][j]; vr,vi=rows[h][j]
                    r=r-(cr*vr-ci*vi); i=i-(cr*vi+ci*vr)
                T[t][h]=(r,i)
    for t in range(nt-1):
        for h in range(2):
            local=lane-(place-128*h)
            above=(local>=8*t+8)&(local<W)
            T[t][h]=tuple(jnp.where(above,0.0,x) for x in T[t][h])
            Z[t][h]=tuple(jnp.where(above,0.0,x) for x in Z[t][h])
    return T,Z
PR=((0,0),(0,1),(1,0),(1,1),(0,2),(2,0))
def invert(ar,ai):
    sub=lax.broadcasted_iota(jnp.int32,S8,0); lane=lax.broadcasted_iota(jnp.int32,S8,1)
    @pl.loop(0,N//W)
    def _(k):
        place=pl.multiple_of(k*W,W)
        old=[ar[pl.ds(place,W),:],ai[pl.ds(place,W),:]]
        T=[[tuple(old[c][8*t:8*t+8,128*h:128*h+128] for c in (0,1)) for h in (0,1)] for t in range(W//8)]
        Y,Z=panel(T,place,sub,lane)
        whole=lambda M: [jnp.concatenate([jnp.concatenate([m[0][c],m[1][c]],1) for m in M],0) for c in (0,1)]
        ys=[split3(u) for u in whole(Y)]; zs=[split3(v) for v in whole(Z)]; ns=[-v for v in zs[1]]
        left=jnp.concatenate([ys[0][a] for a,_ in PR]+[ys[1][a] for a,_ in PR],0)
        re=jnp.concatenate([zs[0][b] for _,b in PR]+[ns[b] for _,b in PR],0)
        im=jnp.concatenate([zs[1][b] for _,b in PR]+[zs[0][b] for _,b in PR],0)
        right=jnp.concatenate([re,im],1)
        out=lax.dot_general(left,right,(((0,),(0,)),((),())),preferred_element_type=jnp.float32)
        full=lax.broadcasted_iota(jnp.int32,(1,N),1)-place
        keep=jnp.broadcast_to((full<0)|(full>=W),(N,N))
        ar[pl.ds(place,W),:]=jnp.zeros((W,N),jnp.float32)
        ai[pl.ds(place,W),:]=jnp.zeros((W,N),jnp.float32)
        ar[...]=jnp.where(keep,ar[...],0.0)-out[:,:N]
        ai[...]=jnp.where(keep,ai[...],0.0)-out[:,N:]


def prep_kernel(flag, got, vecs, out):
    turned = flag[0]
    for b in range(2):
        rows = jnp.concatenate([got[e, 16 * b : 16 * b + 16, :] for e in range(16)], 0)
        hop = LATERAL_SCALE * (rows + rows.T)
        pot = got[0, 32 + b : 33 + b, :]
        for e in range(1, 16):
            pot = pot + got[e, 32 + b : 33 + b, :]
        on_diag = lax.broadcasted_iota(jnp.int32, (N, N), 0) == lax.broadcasted_iota(
            jnp.int32, (N, N), 1
        )
        place = jnp.where(turned == 1, 1 - b, b) * N
        out[pl.ds(pl.multiple_of(place, N), N), :] = jnp.where(on_diag, -pot - hop, -hop)
    out[2 * N : 2 * N + 8, :] = vecs[...]


def row_times(vector, matrix):
    return jnp.dot(vector, matrix, precision=HIGHEST, preferred_element_type=jnp.float32)


def apply(vr, vi, gr, gi):
    both = jnp.concatenate([vr, vi, jnp.zeros((6, N), jnp.float32)], 0)
    a = row_times(both, gr)
    b = row_times(both, gi)
    return b[1:2] - a[0:1], -a[1:2] - b[0:1]


def load_block(ar, ai, real, link, energy):
    across = jnp.broadcast_to(link, (N, N))
    scale = across * across.T
    on_diag = lax.broadcasted_iota(jnp.int32, (N, N), 0) == lax.broadcasted_iota(
        jnp.int32, (N, N), 1
    )
    ar[...] = real + scale * ar[...] + jnp.where(on_diag, energy, 0.0)
    ai[...] = scale * ai[...] + jnp.where(on_diag, BROADENING, 0.0)


def chain_kernel(flag, energy, pack, start, before, mats, vecs, ar, ai, carry):
    ar[...] = start[1, 0]
    ai[...] = start[1, 1]
    carry[...] = before[1]

    @pl.loop(0, 2)
    def _(b):
        here = pack[2 * N : 2 * N + 8, :]
        pick = lambda i: jnp.where(b == 0, here[i : i + 1], here[i + 1 : i + 2])
        bond, src_r, src_i = pick(0), pick(2), pick(4)
        link = jnp.where(flag[0] == 1, bond, carry[3:4, :])
        load_block(ar, ai, pack[pl.ds(pl.multiple_of(b * N, N), N), :], link, energy[0])
        rhs_r = src_r + link * carry[0:1, :]
        rhs_i = src_i + link * carry[1:2, :]
        invert(ar, ai)
        mats[b, 0] = ar[...]
        mats[b, 1] = ai[...]
        q_r, q_i = apply(rhs_r, rhs_i, ar[...], ai[...])
        now = jnp.concatenate(
            [q_r, q_i, link, bond, rhs_r, rhs_i, jnp.zeros((2, N), jnp.float32)], 0
        )
        carry[...] = now
        vecs[b] = now


def last_kernel(
    flag, energy, weight, pack, m0, m1, m2, m3, v0, v1, v2, v3, far_m, far_v, out, ar, ai
):
    all_m = [m0, m1, m2, m3]
    all_v = [v0, v1, v2, v3]
    middle = jnp.where(flag[0] == 1, far_v[3:4, :], v3[1, 3:4, :])
    ar[...] = m3[0, 0]
    ai[...] = m3[0, 1]
    load_block(ar, ai, pack[N : 2 * N, :], v3[1, 2:3, :], energy[0])
    across = jnp.broadcast_to(middle, (N, N))
    scale = across * across.T
    ar[...] = ar[...] + scale * far_m[0]
    ai[...] = ai[...] + scale * far_m[1]
    rhs_r = v3[1, 4:5, :] + middle * far_v[0:1, :]
    rhs_i = v3[1, 5:6, :] + middle * far_v[1:2, :]
    invert(ar, ai)
    now_r, now_i = apply(rhs_r, rhs_i, ar[...], ai[...])
    rows = [weight[0] * (now_r * now_r + now_i * now_i)]
    for j in range(6, -1, -1):
        link = all_v[(j + 1) // 2][(j + 1) % 2, 2:3, :]
        vec = all_v[j // 2]
        b = j % 2
        add_r, add_i = apply(link * now_r, link * now_i, all_m[j // 2][b, 0], all_m[j // 2][b, 1])
        now_r = vec[b, 0:1, :] + add_r
        now_i = vec[b, 1:2, :] + add_i
        rows.append(weight[0] * (now_r * now_r + now_i * now_i))
    out[...] = jnp.concatenate(rows[::-1], 0)


SMEM = pl.BlockSpec(memory_space=pltpu.SMEM)
VMEM = pl.BlockSpec(memory_space=pltpu.VMEM)
PARAMS = pltpu.CompilerParams(vmem_limit_bytes=48 * 2**20)
MATRIX = pltpu.VMEM((N, N), jnp.float32)


def shape(*dims):
    return jax.ShapeDtypeStruct(dims, jnp.float32)


def prep(flag, got, vecs):
    return pl.pallas_call(
        prep_kernel,
        out_shape=shape(PACK, N),
        in_specs=[SMEM, VMEM, VMEM],
        out_specs=VMEM,
        compiler_params=PARAMS,
    )(flag, got, vecs)


def chain(flag, energy, pack, start, before):
    return pl.pallas_call(
        chain_kernel,
        out_shape=[shape(2, 2, N, N), shape(2, 8, N)],
        in_specs=[SMEM, SMEM, VMEM, VMEM, VMEM],
        out_specs=[VMEM, VMEM],
        scratch_shapes=[MATRIX, MATRIX, pltpu.VMEM((8, N), jnp.float32)],
        compiler_params=PARAMS,
    )(flag, energy, pack, start, before)


def last(flag, energy, weight, pack, mats, vecs, far_m, far_v):
    return pl.pallas_call(
        last_kernel,
        out_shape=shape(8, N),
        in_specs=[SMEM] * 3 + [VMEM] * 11,
        out_specs=VMEM,
        scratch_shapes=[MATRIX, MATRIX],
        compiler_params=PARAMS,
    )(flag, energy, weight, pack, *mats, *vecs, far_m, far_v)


def shards(
    occupancy, onsite, defect_shift, site_order, lateral, coupling, energies, weights, sources
):
    slab = lax.axis_index("slab")
    column = lax.axis_index("energy")
    pot_piece = onsite + occupancy.astype(jnp.float32) * defect_shift
    mine = lax.dynamic_slice(site_order, (column * 16,), (16,))
    at = mine[:, None] == lax.broadcasted_iota(jnp.int32, (16, N), 1)
    spread = jnp.sum(jnp.where(at[None], pot_piece[:, :, None], 0.0), axis=1)
    piece = jnp.concatenate([lateral.reshape(32, N), spread, jnp.zeros((6, N), jnp.float32)], 0)
    got = lax.all_to_all(jnp.broadcast_to(piece[None], (16, 40, N)), "energy", 0, 0)
    flip = slab >= 4
    flag = flip.astype(jnp.int32)[None]
    vecs = jnp.stack([coupling, sources[0, 0], sources[1, 0]])
    vecs = jnp.where(flip, vecs[:, ::-1], vecs).reshape(6, N)
    vecs = jnp.concatenate([vecs, jnp.zeros((2, N), jnp.float32)], 0)
    own = prep(flag, got, vecs)
    packs = [
        own,
        lax.ppermute(own, "slab", [(1, 0), (6, 7)]),
        lax.ppermute(own, "slab", [(2, 0), (5, 7)]),
        lax.ppermute(own, "slab", [(3, 0), (4, 7)]),
    ]
    start = jnp.zeros((2, 2, N, N), jnp.float32)
    before = jnp.zeros((2, 8, N), jnp.float32)
    mats, vecs = [], []
    for pack in packs:
        start, before = chain(flag, energies, pack, start, before)
        mats.append(start)
        vecs.append(before)
    swap = [(0, 7), (7, 0)]
    far_m, far_v = lax.ppermute((start[1], before[1]), "slab", swap)
    density = last(flag, energies, weights, packs[3], mats, vecs, far_m, far_v)
    density = jnp.where(flip, density[::-1], density)
    parts = density.reshape(4, 2, 16, 16)
    low = jnp.where(slab == 0, parts, 0.0)
    high = jnp.where(slab == 7, parts, 0.0)
    sent = jnp.concatenate([low, high], 0).transpose(0, 2, 1, 3).reshape(128, 2, 16)
    return jnp.sum(lax.all_to_all(sent, ("slab", "energy"), 0, 0), axis=0)


def solution(mesh):
    return jax.shard_map(
        shards,
        mesh=mesh,
        in_specs=(
            P("slab", "energy"),
            P("slab", "energy"),
            P("slab", "energy"),
            P(),
            P("slab", "energy", None),
            P("slab", None),
            P("energy"),
            P("energy"),
            P(None, "energy", "slab", None),
        ),
        out_specs=P("slab", "energy"),
        check_vma=False,
    )
```

time: 1450 us -> 178 us (0.12); the launches traced: 1420 us -> 178 us
  other arithmetic: 850 us -> 1.72 us
  matrix products: 350 us -> 0 us
  Pallas kernels: 0 us -> 116 us
  waiting for transfers between devices: 79.3 us -> 10.9 us
  blocking collectives: 81.8 us -> 23.9 us
  loops' own time: 15.9 us -> 0 us
  between operations: 16.6 us -> 1.57 us
    another operation x184 -> x1, other arithmetic: 822 us -> 0.01 us  [shards(): vecs = jnp.stack([coupling, sources[0, 0], sources[1, 0]])]
    dot_general x928 -> x0, matrix products: 328 us -> none  [the longest x712 205 us: real_product(): jnp.einsum('ekl,elm->ekm', first_mat, second_mat, precision=HIGHEST, pref...]
    pallas_call x0 -> x6, Pallas kernels: none -> 116 us  [the longest x4 100 us: chain(): pl.pallas_call(chain_kernel, out_shape=[shape(2, 2, N, N), shape(2, 8, N)...]
    all_gather x3 -> x0, waiting for transfers between devices: 54.3 us -> none  [the longest x1 33.8 us: shards(): lax.all_gather(upper[None], 'slab', axis=0, tiled=True)]
    all_gather x3 -> x0, blocking collectives: 48.4 us -> none  [the longest x1 21.3 us: shards(): lax.all_gather(lateral, 'energy', axis=1, tiled=True)]
    unnamed x1 -> x0, blocking collectives: 33.4 us -> none
    ppermute x5, waiting for transfers between devices: 24.2 us -> 0.01 us  [the longest x2 0.01 us: shards(): far_m, far_v = lax.ppermute((start[1], before[1]), 'slab', swap)]
    all_to_all x0 -> x1, blocking collectives: none -> 23.9 us  [shards(): return jnp.sum(lax.all_to_all(sent, ('slab', 'energy'), 0, 0), axis=0)]
  transfers between devices with their start and end apart: 8 -> 6, of which waited for: 6 -> 1; matrix products, arithmetic and copies ran while one was open for 8% -> 0% of each run, Pallas kernels for 0% -> 42%
where the time goes in v1:
time: 178 us
  Pallas kernels  116 us (65%)
  blocking collectives  23.9 us (13%)
  starting transfers between devices  16.3 us (9%)
  waiting for transfers between devices  10.9 us (6%)
  local copies, waits for them, and re-layouts  7.19 us (4%)
    pallas_call x4, Pallas kernels, chain(): pl.pallas_call(chain_kernel, out_shape=[shape(2, 2, N, N), shape(2, 8, N)...  100 us
    all_to_all x1, blocking collectives, shards(): return jnp.sum(lax.all_to_all(sent, ('slab', 'energy'), 0, 0), axis=0)  23.9 us
    pallas_call x1, Pallas kernels, last(): pl.pallas_call(last_kernel, out_shape=shape(8, N), in_specs=[SMEM] * 3 +...  15.8 us
    all_to_all x1, waiting for transfers between devices, shards(): lax.all_to_all(jnp.broadcast_to(piece[None], (16, 40, N)), 'energy', 0, 0)  10.9 us
    all_to_all x1, starting transfers between devices, shards(): lax.all_to_all(jnp.broadcast_to(piece[None], (16, 40, N)), 'energy', 0, 0)  8.73 us
    ppermute x1, starting transfers between devices, shards(): lax.ppermute(own, 'slab', [(1, 0), (6, 7)])  4.06 us
    unnamed x14, local copies, waits for them, and re-layouts  3.93 us
  transfers between devices with their start and end apart: 6, of which 1 were waited for; matrix products, arithmetic and copies ran while one was open for 0% of the time, Pallas kernels for 42%

profile of v1, /device:TPU:1, one launch (start us, length us, event | category | flops | bytes accessed | tf_op | source)
XLA Modules:
  0.0 177.8 jit_solution(9690351982784373062)
XLA Ops:
  0.0 0.0 copy-start.4
  0.0 0.8 dynamic_slice.3
  0.8 0.1 iota_compare_fusion
  0.8 0.7 multiply_add_fusion
  1.6 0.1 select_reduce_fusion
  1.6 0.1 pad.8.clone
  1.7 0.0 copy-done.4
  1.7 0.1 maximum_maximum_fusion
  1.8 0.9 broadcast_in_dim.55
  2.7 0.0 copy-start.6
  2.7 8.7 %all-to-all-start = ((f32[16,40,256]{2,1,0:T(8,128)}), f32[16,40,256]{2,1,0:T(8,128)S(1)}, u32[]{:S(2)}, u32[]{:S(2)}) async-start(f32[16,40,256]{2,1,0:T(8,128)} %broadcast_in_dim.55), calls=%async_computation | async-start | bytes 1310720 | tf_op jit(solution)/shard_map/all_to_all | solution.py:255
  11.4 0.0 copy-done.6
  11.5 0.0 copy-start.5
  11.5 0.7 copy-done.5
  12.1 0.1 rev.6
  12.3 10.9 %all-to-all-done.got = f32[16,40,256]{2,1,0:T(8,128)S(1)} async-done(((f32[16,40,256]{2,1,0:T(8,128)}), f32[16,40,256]{2,1,0:T(8,128)S(1)}, u32[]{:S(2)}, u32[]{:S(2)}) %all-to-all-start) | async-done | bytes 655392 | tf_op jit(solution)/shard_map/all_to_all | solution.py:255
  23.2 0.2 shard_map.91.pack
  23.4 4.1 %collective-permute-start.1 = (f32[520,256]{1,0:T(8,128)S(1)}, f32[520,256]{1,0:T(8,128)S(1)}, u32[]{:S(2)}, u32[]{:S(2)}) collective-permute-start(f32[520,256]{1,0:T(8,128)S(1)} %shard_map.91.pack), channel_id=1, source_target_pairs={{1,0},{6,7},{9,8},{14,15},{17,16},{22,23},{25,24},{30,31},{33,32},... | collective-permute-start | bytes 1597448 | tf_op jit(solution)/shard_map/ppermute | solution.py:264
  27.5 0.7 collective-permute-start.2
  28.2 0.7 collective-permute-start
  29.5 0.1 broadcast_in_dim.56.start
  29.6 25.0 %shard_map.92 = (f32[2,2,256,256]{3,2,1,0:T(8,128)S(1)}, f32[2,8,256]{2,1,0:T(8,128)S(1)}) custom-call(s32[1]{0:T(128)} %bitcast.flag, f32[1]{0:T(128)S(6)} %copy.19.energy, f32[520,256]{1,0:T(8,128)S(1)} %shard_map.91.pack, f32[2,2,256,256]{3,2,1,0:T(8,128)S(1)} %broadcast_in_dim.56.start, f32[2,8,256]{2,1,0:T(8,128)S(1)} %broadcast_in_dim.57.before), custom_call_target="tpu_custom_call" | custom-call | tf_op jit(solution)/shard_map/pallas_call | solution.py:224
  54.7 0.0 collective-permute-done.1.pack
  54.7 25.1 %shard_map.93 = (f32[2,2,256,256]{3,2,1,0:T(8,128)S(1)}, f32[2,8,256]{2,1,0:T(8,128)S(1)}) custom-call(s32[1]{0:T(128)} %bitcast.flag, f32[1]{0:T(128)S(6)} %copy.19.energy, f32[520,256]{1,0:T(8,128)S(1)} %collective-permute-done.1.pack, f32[2,2,256,256]{3,2,1,0:T(8,128)S(1)} %get-tuple-element.13.start.m0, f32[2,8,256]{2,1,0:T(8,128)S(1)} %get-tuple-element.14.before.v0), custom_call_target="tpu_custom_call" | custom-call | tf_op jit(solution)/shard_map/pallas_call | solution.py:224
  79.7 0.0 collective-permute-done.2.pack
  79.7 25.1 %shard_map.94 = (f32[2,2,256,256]{3,2,1,0:T(8,128)S(1)}, f32[2,8,256]{2,1,0:T(8,128)S(1)}) custom-call(s32[1]{0:T(128)} %bitcast.flag, f32[1]{0:T(128)S(6)} %copy.19.energy, f32[520,256]{1,0:T(8,128)S(1)} %collective-permute-done.2.pack, f32[2,2,256,256]{3,2,1,0:T(8,128)S(1)} %get-tuple-element.15.start.m1, f32[2,8,256]{2,1,0:T(8,128)S(1)} %get-tuple-element.16.before.v1), custom_call_target="tpu_custom_call" | custom-call | tf_op jit(solution)/shard_map/pallas_call | solution.py:224
  104.8 0.0 collective-permute-done.pack
  104.8 0.0 copy-start.2
  104.8 25.0 %shard_map.95 = (f32[2,2,256,256]{3,2,1,0:T(8,128)S(1)}, f32[2,8,256]{2,1,0:T(8,128)S(1)}) custom-call(s32[1]{0:T(128)} %bitcast.flag, f32[1]{0:T(128)S(6)} %copy.19.energy, f32[520,256]{1,0:T(8,128)S(1)} %collective-permute-done.pack, f32[2,2,256,256]{3,2,1,0:T(8,128)S(1)} %get-tuple-element.17.start.m2, f32[2,8,256]{2,1,0:T(8,128)S(1)} %get-tuple-element.18.before.v2), custom_call_target="tpu_custom_call" | custom-call | tf_op jit(solution)/shard_map/pallas_call | solution.py:224
  129.9 0.0 copy-done.2
  129.9 0.8 slice_bitcast_fusion
  130.7 1.0 copy-done
  131.7 1.5 collective-permute-start.3
  133.2 0.6 collective-permute-start.4
  134.5 0.0 collective-permute-done.4.far_v
  134.5 0.0 collective-permute-done.3.far_m
  134.5 0.0 copy-start.1
  134.5 1.2 copy-done.1
  135.7 1.0 copy-done.3
  136.8 15.8 %shard_map.96 = f32[8,256]{1,0:T(8,128)S(1)} custom-call(s32[1]{0:T(128)} %bitcast.flag, f32[1]{0:T(128)S(6)} %copy.19.energy, f32[1]{0:T(128)S(6)} %copy.20.weight, f32[520,256]{1,0:T(8,128)S(1)} %copy-done.3, f32[2,2,256,256]{3,2,1,0:T(8,128)S(1)} %get-tuple-element.13.start.m0, f32[2,2,256,256]{3,2,1,0:T(8,128)S(1)} %get-tuple-element.15.start.m1, ...), custom_call_target="tpu_custom_call" | custom-call | tf_op jit(solution)/shard_map/pallas_call | solution.py:235
  152.6 0.1 rev.7
  152.7 0.1 select_n.51
  152.7 0.1 copy.15
  152.8 0.1 select_n.54
  152.9 0.1 copy.16
  153.1 0.1 copy.18
  153.2 23.9 %all_to_all.10 = f32[128,2,16]{2,1,0:T(2,128)S(1)} all-to-all(f32[128,2,16]{2,1,0:T(2,128)S(1)} %bitcast.14), channel_id=1, replica_groups=mesh['energy'=16,'slab'=8] {'slab','energy'}, dimensions={0} | all-to-all | bytes 32768 | tf_op jit(solution)/shard_map/all_to_all | solution.py:283
  177.1 0.7 reduce_sum.19
  (12 shorter events, 0.1 us)
Async XLA Ops:
  0.0 1.7 copy-start.4
  2.7 8.7 %copy-start.6 = (f32[2,1,2,256]{3,2,1,0:T(2,128)S(1)}, f32[2,1,2,256]{3,2,1,0:T(2,128)}, u32[]{:S(2)}) copy-start(f32[2,1,2,256]{3,2,1,0:T(2,128)} %param.17) | copy-start | bytes 12292
  2.7 20.5 %all-to-all-start = ((f32[16,40,256]{2,1,0:T(8,128)}), f32[16,40,256]{2,1,0:T(8,128)S(1)}, u32[]{:S(2)}, u32[]{:S(2)}) async-start(f32[16,40,256]{2,1,0:T(8,128)} %broadcast_in_dim.55), calls=%async_computation | async-start | bytes 1310720 | tf_op jit(solution)/shard_map/all_to_all | solution.py:255
  11.5 0.7 copy-start.5
  23.4 31.3 %collective-permute-start.1 = (f32[520,256]{1,0:T(8,128)S(1)}, f32[520,256]{1,0:T(8,128)S(1)}, u32[]{:S(2)}, u32[]{:S(2)}) collective-permute-start(f32[520,256]{1,0:T(8,128)S(1)} %shard_map.91.pack), channel_id=1, source_target_pairs={{1,0},{6,7},{9,8},{14,15},{17,16},{22,23},{25,24},{30,31},{33,32},... | collective-permute-start | bytes 1597448 | tf_op jit(solution)/shard_map/ppermute | solution.py:264
  27.5 52.3 %collective-permute-start.2 = (f32[520,256]{1,0:T(8,128)S(1)}, f32[520,256]{1,0:T(8,128)S(1)}, u32[]{:S(2)}, u32[]{:S(2)}) collective-permute-start(f32[520,256]{1,0:T(8,128)S(1)} %shard_map.91.pack), channel_id=1, source_target_pairs={{2,0},{5,7},{10,8},{13,15},{18,16},{21,23},{26,24},{29,31},{34,32}... | collective-permute-start | bytes 1597448 | tf_op jit(solution)/shard_map/ppermute | solution.py:265
  28.2 76.6 %collective-permute-start = (f32[520,256]{1,0:T(8,128)S(1)}, f32[520,256]{1,0:T(8,128)S(1)}, u32[]{:S(2)}, u32[]{:S(2)}) collective-permute-start(f32[520,256]{1,0:T(8,128)S(1)} %shard_map.91.pack), channel_id=1, source_target_pairs={{3,0},{4,7},{11,8},{12,15},{19,16},{20,23},{27,24},{28,31},{35,32}... | collective-permute-start | bytes 1597448 | tf_op jit(solution)/shard_map/ppermute | solution.py:266
  104.8 25.1 %copy-start.2 = (f32[520,256]{1,0:T(8,128)}, f32[520,256]{1,0:T(8,128)S(1)}, u32[]{:S(2)}) copy-start(f32[520,256]{1,0:T(8,128)S(1)} %collective-permute-done.pack) | copy-start | bytes 1597444
  130.7 1.0 copy-start
  131.7 2.8 %collective-permute-start.3 = (f32[2,256,256]{2,1,0:T(8,128)}, f32[2,256,256]{2,1,0:T(8,128)}, u32[]{:S(2)}, u32[]{:S(2)}) collective-permute-start(f32[2,256,256]{2,1,0:T(8,128)} %slice_bitcast_fusion), channel_id=1, source_target_pairs={{0,7},{7,0},{8,15},{15,8},{16,23},{23,16},{24,31},{31,24},{32,39},... | collective-permute-start | bytes 1572872 | tf_op jit(solution)/shard_map/ppermute | solution.py:276
  133.2 1.3 collective-permute-start.4
  134.5 1.2 copy-start.1
  135.7 1.0 copy-start.3

commit v2 on v1

v2 whole, which is shorter than its diff:
```python
import functools
import jax
import jax.numpy as jnp
from jax import lax
from jax.experimental import pallas as pl
from jax.experimental.pallas import tpu as pltpu
from jax.sharding import PartitionSpec as P

BROADENING = 1.2
LATERAL_SCALE = 0.9
HIGHEST = lax.Precision.HIGHEST
PACK = 2 * 256 + 8
N=256
W=32
S8=(8,128)
def row(t,s): return jnp.broadcast_to(t[s:s+1],S8)
def lane_of(t,idx): return jnp.take_along_axis(t,idx,axis=1)
def split3(x):
    h=x.astype(jnp.bfloat16); r=x-h.astype(jnp.float32)
    m=r.astype(jnp.bfloat16); l=(r-m.astype(jnp.float32)).astype(jnp.bfloat16)
    return h,m,l
MIX=True
def times(x,y): return (x[0]*y[0]-x[1]*y[1],x[0]*y[1]+x[1]*y[0])
def less(x,a,b): return (x[0]-(a[0]*b[0]-a[1]*b[1]),x[1]-(a[0]*b[1]+a[1]*b[0]))
def row2(x,j): return (row(x[0],j),row(x[1],j))
def panel(T,place,sub,lane):
    half=place//128; off=place-128*half
    nt=W//8
    Z=[]
    for s in range(nt):
        pick=lambda t: tuple(jnp.where(half==0,T[t][0][c],T[t][1][c]) for c in (0,1))
        idx=[jnp.full(S8,off+8*s+j,jnp.int32) for j in range(8)]
        wide=lambda x: [tuple(lane_of(c,idx[j]) for c in x) for j in range(8)]
        C=wide(pick(s))
        O={t:wide(pick(t)) for t in range(s+1,nt)}
        first=place+8*s
        for h in range(2):
            local=lane-(first-128*h)
            inside=(local>=0)&(local<8)
            minus=jnp.where(local==sub,-1.0,0.0)
            for t in range(s,nt):
                r,i=T[t][h]
                T[t][h]=(jnp.where(inside,minus if t==s else 0.0,r),jnp.where(inside,0.0,i))
        X=[T[s][0],T[s][1]]
        Q=None
        rows=[[],[]]
        p=row2(C[0],0)
        for j in range(8):
            inv=1.0/(p[0]*p[0]+p[1]*p[1])
            c=C[j]
            q=(p[0]*inv,-p[1]*inv)
            Q=q if j==0 else tuple(jnp.where(sub==j,a,b) for a,b in zip(q,Q))
            if j<7:
                e=row2(c,j+1)
                g=times(times(e,e),(p[0],-p[1]))
                n=row2(C[j+1],j+1)
                p=(n[0]-g[0]*inv,n[1]-g[1]*inv)
                low=tuple(jnp.where(sub>j,a,0.0) for a in c)
                scaled=times(c,q)
                for j2 in range(j+1,8):
                    w=row2(scaled,j2)
                    C[j2]=less(C[j2],low,w)
                    for t in range(s+1,min(nt,s+2) if MIX else nt): O[t][j2]=less(O[t][j2],O[t][j],w)
            for h in range(2):
                w=times(row2(X[h],j),q)
                rows[h].append(w)
                if j<7: X[h]=less(X[h],low,w)
        T[s]=X
        z=[times(x,Q) for x in X]
        Z.append(z)
        if s<nt-1:
            for h in range(2):
                x=T[s+1][h]
                for j in range(8): x=less(x,O[s+1][j],rows[h][j])
                T[s+1][h]=x
        if s<nt-2:
            if MIX:
                V=list(z)
                for j in range(7,0,-1):
                    u=times(C[j],Q)
                    u=tuple(jnp.where(sub<j,a,0.0) for a in u)
                    V=[less(v,u,row2(v,j)) for v in V]
                rows=[[row2(v,j) for j in range(8)] for v in V]
            for t in range(s+2,nt):
                for h in range(2):
                    x=T[t][h]
                    for j in range(8): x=less(x,O[t][j],rows[h][j])
                    T[t][h]=x
    for t in range(nt-1):
        for h in range(2):
            local=lane-(place-128*h)
            above=(local>=8*t+8)&(local<W)
            T[t][h]=tuple(jnp.where(above,0.0,x) for x in T[t][h])
            Z[t][h]=tuple(jnp.where(above,0.0,x) for x in Z[t][h])
    return T,Z
PR=((0,0),(0,1),(1,0),(1,1),(0,2),(2,0))
def invert(ar,ai):
    sub=lax.broadcasted_iota(jnp.int32,S8,0); lane=lax.broadcasted_iota(jnp.int32,S8,1)
    @pl.loop(0,N//W)
    def _(k):
        place=pl.multiple_of(k*W,W)
        old=[ar[pl.ds(place,W),:],ai[pl.ds(place,W),:]]
        T=[[tuple(old[c][8*t:8*t+8,128*h:128*h+128] for c in (0,1)) for h in (0,1)] for t in range(W//8)]
        Y,Z=panel(T,place,sub,lane)
        whole=lambda M: [jnp.concatenate([jnp.concatenate([m[0][c],m[1][c]],1) for m in M],0) for c in (0,1)]
        ys=[split3(u) for u in whole(Y)]; zs=[split3(v) for v in whole(Z)]; ns=[-v for v in zs[1]]
        left=jnp.concatenate([ys[0][a] for a,_ in PR]+[ys[1][a] for a,_ in PR],0)
        re=jnp.concatenate([zs[0][b] for _,b in PR]+[ns[b] for _,b in PR],0)
        im=jnp.concatenate([zs[1][b] for _,b in PR]+[zs[0][b] for _,b in PR],0)
        right=jnp.concatenate([re,im],1)
        out=lax.dot_general(left,right,(((0,),(0,)),((),())),preferred_element_type=jnp.float32)
        full=lax.broadcasted_iota(jnp.int32,(1,N),1)-place
        keep=jnp.broadcast_to((full<0)|(full>=W),(N,N))
        ar[pl.ds(place,W),:]=jnp.zeros((W,N),jnp.float32)
        ai[pl.ds(place,W),:]=jnp.zeros((W,N),jnp.float32)
        ar[...]=jnp.where(keep,ar[...],0.0)-out[:,:N]
        ai[...]=jnp.where(keep,ai[...],0.0)-out[:,N:]


def prep_kernel(flag, got, vecs, out):
    turned = flag[0]
    for b in range(2):
        rows = jnp.concatenate([got[e, 16 * b : 16 * b + 16, :] for e in range(16)], 0)
        hop = LATERAL_SCALE * (rows + rows.T)
        pot = got[0, 32 + b : 33 + b, :]
        for e in range(1, 16):
            pot = pot + got[e, 32 + b : 33 + b, :]
        on_diag = lax.broadcasted_iota(jnp.int32, (N, N), 0) == lax.broadcasted_iota(
            jnp.int32, (N, N), 1
        )
        place = jnp.where(turned == 1, 1 - b, b) * N
        out[pl.ds(pl.multiple_of(place, N), N), :] = jnp.where(on_diag, -pot - hop, -hop)
    out[2 * N : 2 * N + 8, :] = vecs[...]


def row_times(vector, matrix):
    return jnp.dot(vector, matrix, precision=HIGHEST, preferred_element_type=jnp.float32)


def apply(vr, vi, gr, gi):
    both = jnp.concatenate([vr, vi, jnp.zeros((6, N), jnp.float32)], 0)
    a = row_times(both, gr)
    b = row_times(both, gi)
    return b[1:2] - a[0:1], -a[1:2] - b[0:1]


def load_block(ar, ai, real, link, energy):
    scale = outer_square(link)
    on_diag = lax.broadcasted_iota(jnp.int32, (N, N), 0) == lax.broadcasted_iota(
        jnp.int32, (N, N), 1
    )
    ar[...] = real + scale * ar[...] + jnp.where(on_diag, energy, 0.0)
    ai[...] = scale * ai[...] + jnp.where(on_diag, BROADENING, 0.0)


def outer_square(link):
    down = jnp.broadcast_to(link, (128, N)).T
    return jnp.concatenate([down, down], 1) * link


def eliminate(flag, energy, here, b, real, ar, ai, carry, mats, vecs, slot):
    pick = lambda i: jnp.where(b == 0, here[i : i + 1], here[i + 1 : i + 2])
    bond, src_r, src_i = pick(0), pick(2), pick(4)
    link = jnp.where(flag[0] == 1, bond, carry[3:4, :])
    load_block(ar, ai, real, link, energy[0])
    rhs_r = src_r + link * carry[0:1, :]
    rhs_i = src_i + link * carry[1:2, :]
    if mats is None:
        return link, bond, rhs_r, rhs_i
    invert(ar, ai)
    mats[slot, 0] = ar[...]
    mats[slot, 1] = ai[...]
    q_r, q_i = apply(rhs_r, rhs_i, ar[...], ai[...])
    now = jnp.concatenate([q_r, q_i, link, bond, jnp.zeros((4, N), jnp.float32)], 0)
    carry[...] = now
    vecs[slot] = now


def first_kernel(flag, energy, pack, mats, vecs, ar, ai, carry):
    ar[...] = jnp.zeros((N, N), jnp.float32)
    ai[...] = jnp.zeros((N, N), jnp.float32)
    carry[...] = jnp.zeros((8, N), jnp.float32)

    @pl.loop(0, 2)
    def _(b):
        real = pack[pl.ds(pl.multiple_of(b * N, N), N), :]
        here = pack[2 * N : 2 * N + 8, :]
        eliminate(flag, energy, here, b, real, ar, ai, carry, mats, vecs, b)


def middle_kernel(
    flag, energy, pack1, pack2, pack3, start, before, mats, vecs, ready, ar, ai, carry, hop, side
):
    ar[...] = start[1, 0]
    ai[...] = start[1, 1]
    carry[...] = before[1]
    for i, pack in enumerate((pack1, pack2, pack3)):
        hop[2 * i] = pack[0:N, :]
        hop[2 * i + 1] = pack[N : 2 * N, :]
        side[i] = pack[2 * N : 2 * N + 8, :]

    @pl.loop(0, 5)
    def _(j):
        b = lax.rem(j, 2)
        eliminate(flag, energy, side[j // 2], b, hop[j], ar, ai, carry, mats, vecs, j)

    link, bond, rhs_r, rhs_i = eliminate(
        flag, energy, side[2], 1, hop[5], ar, ai, carry, None, None, None
    )
    ready[0:N, :] = ar[...]
    ready[N : 2 * N, :] = ai[...]
    ready[2 * N : 2 * N + 8, :] = jnp.concatenate(
        [rhs_r, rhs_i, link, bond, jnp.zeros((4, N), jnp.float32)], 0
    )


def inner_kernel(ready, mat, vec, ar, ai):
    ar[...] = ready[0:N, :]
    ai[...] = ready[N : 2 * N, :]
    side = ready[2 * N : 2 * N + 8, :]
    invert(ar, ai)
    mat[0] = ar[...]
    mat[1] = ai[...]
    q_r, q_i = apply(side[0:1], side[1:2], ar[...], ai[...])
    vec[...] = jnp.concatenate([q_r, q_i, side[2:8]], 0)


def last_kernel(flag, weight, far, m0, v0, m1, v1, m7, v7, out, ar, ai):
    all_m = [m0.at[0], m0.at[1]] + [m1.at[j] for j in range(5)]
    all_v = [v0[0], v0[1]] + [v1[j] for j in range(5)]
    side = far[2 * N : 2 * N + 8, :]
    own = v7[...]
    middle = jnp.where(flag[0] == 1, side[3:4], own[3:4])
    scale = outer_square(middle)
    ar[...] = far[0:N, :] + scale * m7[0]
    ai[...] = far[N : 2 * N, :] + scale * m7[1]
    rhs_r = side[0:1] + middle * own[0:1]
    rhs_i = side[1:2] + middle * own[1:2]
    invert(ar, ai)
    now_r, now_i = apply(rhs_r, rhs_i, ar[...], ai[...])
    rows = []
    link = middle
    for mat, vec in [(m7, own)] + [(all_m[j], all_v[j]) for j in range(6, -1, -1)]:
        add_r, add_i = apply(link * now_r, link * now_i, mat[0], mat[1])
        now_r = vec[0:1] + add_r
        now_i = vec[1:2] + add_i
        rows.append(weight[0] * (now_r * now_r + now_i * now_i))
        link = vec[2:3]
    turned = flag[0] == 1
    low, high = rows[::-1], rows
    out[...] = jnp.where(turned, jnp.concatenate(high, 0), jnp.concatenate(low, 0))


SMEM = pl.BlockSpec(memory_space=pltpu.SMEM)
VMEM = pl.BlockSpec(memory_space=pltpu.VMEM)
PARAMS = pltpu.CompilerParams(vmem_limit_bytes=48 * 2**20)
MATRIX = pltpu.VMEM((N, N), jnp.float32)
SIDE = pltpu.VMEM((8, N), jnp.float32)


def shape(*dims):
    return jax.ShapeDtypeStruct(dims, jnp.float32)


def call(kernel, scalars, arrays, outs, scratch, steps=1):
    return pl.pallas_call(
        kernel,
        out_shape=outs,
        in_specs=[SMEM] * len(scalars) + [VMEM] * len(arrays),
        out_specs=jax.tree.map(lambda _: VMEM, outs),
        scratch_shapes=scratch,
        compiler_params=PARAMS,
        cost_estimate=pl.CostEstimate(
            flops=steps * 8 * N**3, bytes_accessed=steps * 4 * N * N, transcendentals=0
        ),
    )(*scalars, *arrays)


def shards(
    occupancy, onsite, defect_shift, site_order, lateral, coupling, energies, weights, sources
):
    slab = lax.axis_index("slab")
    column = lax.axis_index("energy")
    pot_piece = onsite + occupancy.astype(jnp.float32) * defect_shift
    mine = lax.dynamic_slice(site_order, (column * 16,), (16,))
    at = mine[:, None] == lax.broadcasted_iota(jnp.int32, (16, N), 1)
    spread = jnp.sum(jnp.where(at[None], pot_piece[:, :, None], 0.0), axis=1)
    piece = jnp.concatenate([lateral.reshape(32, N), spread, jnp.zeros((6, N), jnp.float32)], 0)
    got = lax.all_to_all(jnp.broadcast_to(piece[None], (16, 40, N)), "energy", 0, 0)
    flip = slab >= 4
    flag = flip.astype(jnp.int32)[None]
    vecs = jnp.stack([coupling, sources[0, 0], sources[1, 0]])
    vecs = jnp.where(flip, vecs[:, ::-1], vecs).reshape(6, N)
    vecs = jnp.concatenate([vecs, jnp.zeros((2, N), jnp.float32)], 0)
    own = call(prep_kernel, [flag], [got, vecs], shape(PACK, N), [])
    packs = [
        lax.ppermute(own, "slab", [(1, 0), (6, 7)]),
        lax.ppermute(own, "slab", [(2, 0), (5, 7)]),
        lax.ppermute(own, "slab", [(3, 0), (4, 7)]),
    ]
    scalars = [flag, energies]
    m0, v0 = call(
        first_kernel,
        scalars,
        [own],
        [shape(2, 2, N, N), shape(2, 8, N)],
        [MATRIX, MATRIX, SIDE],
        2,
    )
    m1, v1, ready = call(
        middle_kernel,
        scalars,
        packs + [m0, v0],
        [shape(5, 2, N, N), shape(5, 8, N), shape(PACK, N)],
        [MATRIX, MATRIX, SIDE, pltpu.VMEM((6, N, N), jnp.float32), pltpu.VMEM((3, 8, N), jnp.float32)],
        5,
    )
    far = lax.ppermute(ready, "slab", [(0, 7), (7, 0)])
    m7, v7 = call(
        inner_kernel, [], [ready], [shape(2, N, N), shape(8, N)], [MATRIX, MATRIX]
    )
    density = call(
        last_kernel,
        [flag, weights],
        [far, m0, v0, m1, v1, m7, v7],
        shape(8, N),
        [MATRIX, MATRIX],
    )
    parts = density.reshape(4, 2, 16, 16)
    low = jnp.where(slab == 0, parts, 0.0)
    high = jnp.where(slab == 7, parts, 0.0)
    sent = jnp.concatenate([low, high], 0).transpose(0, 2, 1, 3).reshape(128, 2, 16)
    return jnp.sum(lax.all_to_all(sent, ("slab", "energy"), 0, 0), axis=0)


def solution(mesh):
    return jax.shard_map(
        shards,
        mesh=mesh,
        in_specs=(
            P("slab", "energy"),
            P("slab", "energy"),
            P("slab", "energy"),
            P(),
            P("slab", "energy", None),
            P("slab", None),
            P("energy"),
            P("energy"),
            P(None, "energy", "slab", None),
        ),
        out_specs=P("slab", "energy"),
        check_vma=False,
    )
```

time: 178 us -> 156 us (0.88)
  Pallas kernels: 116 us -> 103 us
  blocking collectives: 23.9 us -> 17.1 us
  other arithmetic: 1.72 us -> 3.84 us
    pallas_call x6 -> x5, Pallas kernels: 116 us -> 103 us  [call(): pl.pallas_call(kernel, out_shape=outs, in_specs=[SMEM] * len(scalars) + [...]
    all_to_all x1, blocking collectives: 23.9 us -> 17.1 us  [shards(): return jnp.sum(lax.all_to_all(sent, ('slab', 'energy'), 0, 0), axis=0)]
    unnamed x14 -> x4, local copies, waits for them, and re-layouts: 3.93 us -> 3.25 us
  transfers between devices with their start and end apart: 6 -> 5, of which waited for: 1 -> 1; matrix products, arithmetic and copies ran while one was open for 0% -> 1% of each run, Pallas kernels for 42% -> 21%
where the time goes in v2:
time: 156 us
  Pallas kernels  103 us (66%)
  blocking collectives  17.1 us (11%)
  starting transfers between devices  14.7 us (9%)
  waiting for transfers between devices  9.6 us (6%)
  local copies, waits for them, and re-layouts  6.21 us (4%)
  other arithmetic  3.84 us (2%)
    pallas_call x5, Pallas kernels, call(): pl.pallas_call(kernel, out_shape=outs, in_specs=[SMEM] * len(scalars) + [...  103 us
    all_to_all x1, blocking collectives, shards(): return jnp.sum(lax.all_to_all(sent, ('slab', 'energy'), 0, 0), axis=0)  17.1 us
    all_to_all x1, waiting for transfers between devices, shards(): lax.all_to_all(jnp.broadcast_to(piece[None], (16, 40, N)), 'energy', 0, 0)  9.58 us
    all_to_all x1, starting transfers between devices, shards(): lax.all_to_all(jnp.broadcast_to(piece[None], (16, 40, N)), 'energy', 0, 0)  8.6 us
    ppermute x1, starting transfers between devices, shards(): lax.ppermute(own, 'slab', [(1, 0), (6, 7)])  4.06 us
    unnamed x4, local copies, waits for them, and re-layouts  3.25 us
  transfers between devices with their start and end apart: 5, of which 1 were waited for; matrix products, arithmetic and copies ran while one was open for 1% of the time, Pallas kernels for 21%

profile of v2, /device:TPU:1, one launch (start us, length us, event | category | flops | bytes accessed | tf_op | source)
XLA Modules:
  0.0 155.7 jit_solution(18434682642675654576)
XLA Ops:
  0.0 0.8 dynamic_slice.3
  0.8 0.1 iota_compare_fusion
  0.8 0.7 multiply_add_fusion
  1.5 0.1 select_reduce_fusion
  1.6 0.1 pad.8.clone
  1.7 0.8 maximum_maximum_fusion
  2.5 0.9 broadcast_in_dim.49
  3.4 8.6 %all-to-all-start = ((f32[16,40,256]{2,1,0:T(8,128)}), f32[16,40,256]{2,1,0:T(8,128)S(1)}, u32[]{:S(2)}, u32[]{:S(2)}) async-start(f32[16,40,256]{2,1,0:T(8,128)} %broadcast_in_dim.49), calls=%async_computation | async-start | bytes 1310720 | tf_op jit(solution)/shard_map/all_to_all | solution.py:289
  12.0 0.7 slice_bitcast_fusion.1
  12.7 0.7 pad_maximum_fusion
  13.4 0.1 rev.3
  13.5 0.7 broadcast_select_fusion
  14.2 9.6 %all-to-all-done.got = f32[16,40,256]{2,1,0:T(8,128)S(1)} async-done(((f32[16,40,256]{2,1,0:T(8,128)}), f32[16,40,256]{2,1,0:T(8,128)S(1)}, u32[]{:S(2)}, u32[]{:S(2)}) %all-to-all-start) | async-done | bytes 655392 | tf_op jit(solution)/shard_map/all_to_all | solution.py:289
  23.8 0.2 shard_map.91.pack
  24.0 4.1 %collective-permute-start = (f32[520,256]{1,0:T(8,128)S(1)}, f32[520,256]{1,0:T(8,128)S(1)}, u32[]{:S(2)}, u32[]{:S(2)}) collective-permute-start(f32[520,256]{1,0:T(8,128)S(1)} %shard_map.91.pack), channel_id=1, source_target_pairs={{1,0},{6,7},{9,8},{14,15},{17,16},{22,23},{25,24},{30,31},{33,32},... | collective-permute-start | bytes 1597448 | tf_op jit(solution)/shard_map/ppermute | solution.py:297
  28.1 0.7 collective-permute-start.1
  28.8 0.7 collective-permute-start.2
  30.1 22.2 %shard_map.92 = (f32[2,2,256,256]{3,2,1,0:T(8,128)S(1)}, f32[2,8,256]{2,1,0:T(8,128)S(1)}) custom-call(s32[1]{0:T(128)} %bitcast.flag, f32[1]{0:T(128)S(6)} %copy.19.energy, f32[520,256]{1,0:T(8,128)S(1)} %shard_map.91.pack), custom_call_target="tpu_custom_call" | custom-call | flops 268435456 | bytes 524288 | tf_op jit(solution)/shard_map/pallas_call | solution.py:266
  52.4 0.0 collective-permute-done.pack1
  52.4 0.0 collective-permute-done.1.pack2
  52.4 0.0 collective-permute-done.2.pack3
  52.4 55.7 %shard_map.93 = (f32[5,2,256,256]{3,2,1,0:T(8,128)S(1)}, f32[5,8,256]{2,1,0:T(8,128)S(1)}, f32[520,256]{1,0:T(8,128)S(1)}) custom-call(s32[1]{0:T(128)} %bitcast.flag, f32[1]{0:T(128)S(6)} %copy.19.energy, f32[520,256]{1,0:T(8,128)S(1)} %collective-permute-done.pack1, f32[520,256]{1,0:T(8,128)S(1)} %collective-permute-done.1.pack2, ...), custom_call_target="tpu_custom_call" | custom-call | flops 671088640 | bytes 1310720 | tf_op jit(solution)/shard_map/pallas_call | solution.py:266
  108.1 0.0 copy-start
  108.1 1.5 copy-done
  109.6 0.7 collective-permute-start.3
  110.9 11.0 %shard_map.94 = (f32[2,256,256]{2,1,0:T(8,128)S(1)}, f32[8,256]{1,0:T(8,128)S(1)}) custom-call(f32[520,256]{1,0:T(8,128)S(1)} %get-tuple-element.14.ready), custom_call_target="tpu_custom_call" | custom-call | flops 134217728 | bytes 262144 | tf_op jit(solution)/shard_map/pallas_call | solution.py:266
  121.9 0.0 collective-permute-done.3.far
  121.9 0.0 copy-start.1
  122.0 1.7 %copy-done.1 = f32[5,2,256,256]{3,2,1,0:T(8,128)S(1)} copy-done((f32[5,2,256,256]{3,2,1,0:T(8,128)S(1)}, f32[5,2,256,256]{3,2,1,0:T(8,128)}, u32[]{:S(2)}) %copy-start.1) | copy-done | bytes 2621464
  123.7 13.6 %shard_map.95 = f32[8,256]{1,0:T(8,128)S(1)} custom-call(s32[1]{0:T(128)} %bitcast.flag, f32[1]{0:T(128)S(6)} %copy.20.weight, f32[520,256]{1,0:T(8,128)S(1)} %collective-permute-done.3.far, f32[2,2,256,256]{3,2,1,0:T(8,128)S(1)} %get-tuple-element.12.start.m0, f32[2,8,256]{2,1,0:T(8,128)S(1)} %get-tuple-element.13.before.v0, ...), custom_call_target="tpu_custom_call" | custom-call | flops 134217728 | bytes 262144 | tf_op jit(solution)/shard_map/pallas_call | solution.py:266
  137.3 0.1 select_n.41
  137.4 0.1 copy.15
  137.5 0.1 select_n.44
  137.6 0.1 copy.16
  137.8 0.1 copy.18
  137.9 17.1 %all_to_all.10 = f32[128,2,16]{2,1,0:T(2,128)S(1)} all-to-all(f32[128,2,16]{2,1,0:T(2,128)S(1)} %bitcast.10), channel_id=1, replica_groups=mesh['energy'=16,'slab'=8] {'slab','energy'}, dimensions={0} | all-to-all | bytes 32768 | tf_op jit(solution)/shard_map/all_to_all | solution.py:333
  155.0 0.7 reduce_sum.19
  (5 shorter events, 0.1 us)
Async XLA Ops:
  3.4 20.4 %all-to-all-start = ((f32[16,40,256]{2,1,0:T(8,128)}), f32[16,40,256]{2,1,0:T(8,128)S(1)}, u32[]{:S(2)}, u32[]{:S(2)}) async-start(f32[16,40,256]{2,1,0:T(8,128)} %broadcast_in_dim.49), calls=%async_computation | async-start | bytes 1310720 | tf_op jit(solution)/shard_map/all_to_all | solution.py:289
  24.0 28.3 %collective-permute-start = (f32[520,256]{1,0:T(8,128)S(1)}, f32[520,256]{1,0:T(8,128)S(1)}, u32[]{:S(2)}, u32[]{:S(2)}) collective-permute-start(f32[520,256]{1,0:T(8,128)S(1)} %shard_map.91.pack), channel_id=1, source_target_pairs={{1,0},{6,7},{9,8},{14,15},{17,16},{22,23},{25,24},{30,31},{33,32},... | collective-permute-start | bytes 1597448 | tf_op jit(solution)/shard_map/ppermute | solution.py:297
  28.1 24.3 %collective-permute-start.1 = (f32[520,256]{1,0:T(8,128)S(1)}, f32[520,256]{1,0:T(8,128)S(1)}, u32[]{:S(2)}, u32[]{:S(2)}) collective-permute-start(f32[520,256]{1,0:T(8,128)S(1)} %shard_map.91.pack), channel_id=1, source_target_pairs={{2,0},{5,7},{10,8},{13,15},{18,16},{21,23},{26,24},{29,31},{34,32}... | collective-permute-start | bytes 1597448 | tf_op jit(solution)/shard_map/ppermute | solution.py:298
  28.8 23.6 %collective-permute-start.2 = (f32[520,256]{1,0:T(8,128)S(1)}, f32[520,256]{1,0:T(8,128)S(1)}, u32[]{:S(2)}, u32[]{:S(2)}) collective-permute-start(f32[520,256]{1,0:T(8,128)S(1)} %shard_map.91.pack), channel_id=1, source_target_pairs={{3,0},{4,7},{11,8},{12,15},{19,16},{20,23},{27,24},{28,31},{35,32}... | collective-permute-start | bytes 1597448 | tf_op jit(solution)/shard_map/ppermute | solution.py:299
  108.1 1.5 copy-start
  109.6 12.3 %collective-permute-start.3 = (f32[520,256]{1,0:T(8,128)S(1)}, f32[520,256]{1,0:T(8,128)S(1)}, u32[]{:S(2)}, u32[]{:S(2)}) collective-permute-start(f32[520,256]{1,0:T(8,128)S(1)} %get-tuple-element.14.ready), channel_id=1, source_target_pairs={{0,7},{7,0},{8,15},{15,8},{16,23},{23,16},{24,31},{31,24},{32,39},... | collective-permute-start | bytes 1597448 | tf_op jit(solution)/shard_map/ppermute | solution.py:318
  121.9 1.7 %copy-start.1 = (f32[5,2,256,256]{3,2,1,0:T(8,128)S(1)}, f32[5,2,256,256]{3,2,1,0:T(8,128)}, u32[]{:S(2)}) copy-start(f32[5,2,256,256]{3,2,1,0:T(8,128)} %copy-done) | copy-start | bytes 7864324

commit v3 on v2

--- a/solution.py
+++ b/solution.py
@@ -133,84 +133,214 @@
     out[2 * N : 2 * N + 8, :] = vecs[...]
 
 
-def row_times(vector, matrix):
-    return jnp.dot(vector, matrix, precision=HIGHEST, preferred_element_type=jnp.float32)
-
-
-def apply(vr, vi, gr, gi):
-    both = jnp.concatenate([vr, vi, jnp.zeros((6, N), jnp.float32)], 0)
-    a = row_times(both, gr)
-    b = row_times(both, gi)
-    return b[1:2] - a[0:1], -a[1:2] - b[0:1]
+def row_times(vector, matrix, turned=False):
+    return lax.dot_general(
+        vector,
+        matrix,
+        (((1,), (1 if turned else 0,)), ((), ())),
+        precision=HIGHEST,
+        preferred_element_type=jnp.float32,
+    )
+
+
+def apply(v, gr, gi, turned=False):
+    both = jnp.concatenate([v[0], v[1], jnp.zeros((6, N), jnp.float32)], 0)
+    a = row_times(both, gr, turned)
+    b = row_times(both, gi, turned)
+    return a[0:1] - b[1:2], a[1:2] + b[0:1]
+
+
+def product(a, b, turned=False):
+    axis = 0 if turned else 1
+    a3 = [split3(a[0]), split3(a[1])]
+    b3 = [split3(b[0]), split3(b[1])]
+    out_r = out_i = 0.0
+    for i, j in PR[::-1]:
+        left = jnp.concatenate([a3[0][i], a3[1][i]], axis)
+        right = jnp.concatenate(
+            [
+                jnp.concatenate([b3[0][j], b3[1][j]], 1),
+                jnp.concatenate([-b3[1][j], b3[0][j]], 1),
+            ],
+            0,
+        )
+        out = lax.dot_general(
+            left, right, (((axis,), (0,)), ((), ())), preferred_element_type=jnp.float32
+        )
+        out_r = out_r + out[:, :N]
+        out_i = out_i + out[:, N:]
+    return out_r, out_i
+
+
+def on_diagonal():
+    return lax.broadcasted_iota(jnp.int32, (N, N), 0) == lax.broadcasted_iota(
+        jnp.int32, (N, N), 1
+    )
+
+
+def down(link):
+    tall = jnp.broadcast_to(link, (128, N)).T
+    return jnp.concatenate([tall, tall], 1)
 
 
 def load_block(ar, ai, real, link, energy):
-    scale = outer_square(link)
-    on_diag = lax.broadcasted_iota(jnp.int32, (N, N), 0) == lax.broadcasted_iota(
-        jnp.int32, (N, N), 1
-    )
-    ar[...] = real + scale * ar[...] + jnp.where(on_diag, energy, 0.0)
-    ai[...] = scale * ai[...] + jnp.where(on_diag, BROADENING, 0.0)
-
-
-def outer_square(link):
-    down = jnp.broadcast_to(link, (128, N)).T
-    return jnp.concatenate([down, down], 1) * link
-
-
-def eliminate(flag, energy, here, b, real, ar, ai, carry, mats, vecs, slot):
-    pick = lambda i: jnp.where(b == 0, here[i : i + 1], here[i + 1 : i + 2])
-    bond, src_r, src_i = pick(0), pick(2), pick(4)
+    scale = down(link) * link
+    diag = on_diagonal()
+    ar[...] = real + scale * ar[...] + jnp.where(diag, energy, 0.0)
+    ai[...] = scale * ai[...] + jnp.where(diag, BROADENING, 0.0)
+
+
+def eliminate(flag, energy, bond, source, real, ar, ai, carry, mats, vecs, slot):
     link = jnp.where(flag[0] == 1, bond, carry[3:4, :])
     load_block(ar, ai, real, link, energy[0])
-    rhs_r = src_r + link * carry[0:1, :]
-    rhs_i = src_i + link * carry[1:2, :]
-    if mats is None:
-        return link, bond, rhs_r, rhs_i
+    rhs = (source[0] + link * carry[0:1, :], source[1] + link * carry[1:2, :])
     invert(ar, ai)
     mats[slot, 0] = ar[...]
     mats[slot, 1] = ai[...]
-    q_r, q_i = apply(rhs_r, rhs_i, ar[...], ai[...])
-    now = jnp.concatenate([q_r, q_i, link, bond, jnp.zeros((4, N), jnp.float32)], 0)
+    q_r, q_i = apply(rhs, ar[...], ai[...])
+    now = jnp.concatenate([-q_r, -q_i, link, bond, jnp.zeros((4, N), jnp.float32)], 0)
     carry[...] = now
     vecs[slot] = now
 
 
-def first_kernel(flag, energy, pack, mats, vecs, ar, ai, carry):
+def fold(one, two):
+    row_id = lax.broadcasted_iota(jnp.int32, (N, N), 0)
+    lane_id = lax.broadcasted_iota(jnp.int32, (N, N), 1)
+    diag = jnp.sum(jnp.where(row_id == lane_id, two, 0.0), axis=0, keepdims=True)
+    return jnp.where(row_id >= lane_id, one, two), diag
+
+
+def unfold(both, diag):
+    row_id = lax.broadcasted_iota(jnp.int32, (N, N), 0)
+    lane_id = lax.broadcasted_iota(jnp.int32, (N, N), 1)
+    other = both.T
+    one = jnp.where(row_id >= lane_id, both, other)
+    two = jnp.where(row_id < lane_id, both, jnp.where(row_id == lane_id, diag, other))
+    return one, two
+
+
+def first_kernel(flag, inner, energy, own, after, mats, vecs, mid, ar, ai, carry, hop, side):
     ar[...] = jnp.zeros((N, N), jnp.float32)
     ai[...] = jnp.zeros((N, N), jnp.float32)
     carry[...] = jnp.zeros((8, N), jnp.float32)
+    first = own[2 * N : 2 * N + 8, :]
+    second = after[2 * N : 2 * N + 8, :]
+    is_inner = inner[0] == 1
+    hop[0] = jnp.where(is_inner, own[N : 2 * N, :], own[0:N, :])
+    hop[1] = jnp.where(is_inner, after[0:N, :], own[N : 2 * N, :])
+    rows = lambda m, b: jnp.concatenate([m[b : b + 1], m[2 + b : 3 + b], m[4 + b : 5 + b]] * 2, 0)
+    side[0, 0:6] = jnp.where(is_inner, rows(first, 1), rows(first, 0))
+    side[1, 0:6] = jnp.where(is_inner, rows(second, 0), rows(first, 1))
 
     @pl.loop(0, 2)
     def _(b):
-        real = pack[pl.ds(pl.multiple_of(b * N, N), N), :]
-        here = pack[2 * N : 2 * N + 8, :]
-        eliminate(flag, energy, here, b, real, ar, ai, carry, mats, vecs, b)
-
-
-def middle_kernel(
-    flag, energy, pack1, pack2, pack3, start, before, mats, vecs, ready, ar, ai, carry, hop, side
-):
+        here = side[b]
+        eliminate(
+            flag, energy, here[0:1], (here[1:2], here[2:3]), hop[b], ar, ai, carry, mats, vecs, b
+        )
+
+    @pl.when(is_inner)
+    def _():
+        link = carry[2:3, :]
+        n5 = (mats[0, 0], mats[0, 1])
+        n6 = (mats[1, 0], mats[1, 1])
+        m56 = product((n5[0] * link, n5[1] * link), n6)
+        m55 = product((m56[0] * link, m56[1] * link), n5)
+        m55 = (-n5[0] - m55[0], -n5[1] - m55[1])
+        m66 = (-n6[0], -n6[1])
+        folded = [fold(*m55), fold(*m66), fold(own[0:N, :], after[N : 2 * N, :])]
+        mid[0:N, :] = m56[0]
+        mid[N : 2 * N, :] = m56[1]
+        for i in range(3):
+            mid[(2 + i) * N : (3 + i) * N, :] = folded[i][0]
+        s5 = (side[0, 1:2, :], side[0, 2:3, :])
+        s6 = (side[1, 1:2, :], side[1, 2:3, :])
+        a = apply(s5, *m55)
+        b = apply(s6, *m56, turned=True)
+        c = apply(s5, *m56)
+        d = apply(s6, *m66)
+        zero = jnp.zeros((1, N), jnp.float32)
+        mid[5 * N : 5 * N + 8, :] = jnp.concatenate(
+            [a[0] + b[0], a[1] + b[1], c[0] + d[0], c[1] + d[1]]
+            + [folded[i][1] for i in range(3)]
+            + [zero],
+            0,
+        )
+        mid[5 * N + 8 : 5 * N + 16, :] = first
+        mid[5 * N + 16 : 5 * N + 24, :] = second
+
+
+def second_kernel(flag, energy, after, start, before, mats, vecs, ar, ai, carry, side):
     ar[...] = start[1, 0]
     ai[...] = start[1, 1]
     carry[...] = before[1]
-    for i, pack in enumerate((pack1, pack2, pack3)):
-        hop[2 * i] = pack[0:N, :]
-        hop[2 * i + 1] = pack[N : 2 * N, :]
-        side[i] = pack[2 * N : 2 * N + 8, :]
-
-    @pl.loop(0, 5)
-    def _(j):
-        b = lax.rem(j, 2)
-        eliminate(flag, energy, side[j // 2], b, hop[j], ar, ai, carry, mats, vecs, j)
-
-    link, bond, rhs_r, rhs_i = eliminate(
-        flag, energy, side[2], 1, hop[5], ar, ai, carry, None, None, None
-    )
-    ready[0:N, :] = ar[...]
-    ready[N : 2 * N, :] = ai[...]
+    have = after[2 * N : 2 * N + 8, :]
+    for b in range(2):
+        side[b, 0:3] = jnp.concatenate(
+            [have[b : b + 1], have[2 + b : 3 + b], have[4 + b : 5 + b]], 0
+        )
+
+    @pl.loop(0, 2)
+    def _(b):
+        here = side[b]
+        real = after[pl.ds(pl.multiple_of(b * N, N), N), :]
+        eliminate(
+            flag, energy, here[0:1], (here[1:2], here[2:3]), real, ar, ai, carry, mats, vecs, b
+        )
+
+
+def third_kernel(flag, energy, start, before, mid, mat, vec, ready, ar, ai):
+    p2 = mid[5 * N + 8 : 5 * N + 16, :]
+    p3 = mid[5 * N + 16 : 5 * N + 24, :]
+    back = flag[0] == 1
+    link = jnp.where(back, p2[0:1], before[1, 3:4, :])
+    c4 = jnp.where(back, p2[1:2], p2[0:1])
+    c6 = jnp.where(back, p3[1:2], p3[0:1])
+    t = mid[5 * N : 5 * N + 8, :]
+    ar[...] = start[1, 0]
+    ai[...] = start[1, 1]
+    a4, a7 = unfold(mid[4 * N : 5 * N, :], t[6:7])
+    m55 = unfold(mid[2 * N : 3 * N, :], t[4:5])
+    m66 = unfold(mid[3 * N : 4 * N, :], t[5:6])
+    load_block(ar, ai, a4, link, energy[0])
+    down4 = down(c4)
+    square = down4 * c4
+    ar[...] = ar[...] - square * m55[0]
+    ai[...] = ai[...] - square * m55[1]
+    rhs = (
+        p2[2:3] + link * before[1, 0:1, :] + c4 * t[0:1],
+        p2[4:5] + link * before[1, 1:2, :] + c4 * t[1:2],
+    )
+    invert(ar, ai)
+    mat[0] = ar[...]
+    mat[1] = ai[...]
+    n_r, n_i = apply(rhs, ar[...], ai[...])
+    q = (-n_r, -n_i)
+    vec[...] = jnp.concatenate([q[0], q[1], link, c4, c6, jnp.zeros((3, N), jnp.float32)], 0)
+    cross = down4 * c6
+    ready[0:N, :] = cross * mid[0:N, :]
+    ready[N : 2 * N, :] = cross * mid[N : 2 * N, :]
+    k = (ready[0:N, :], ready[N : 2 * N, :])
+    x = product((ar[...], ai[...]), k)
+    y = product(k, x, turned=True)
+    onto = apply(q, *k)
+    square = down(c6) * c6
+    diag = on_diagonal()
+    ready[0:N, :] = (
+        a7 + jnp.where(diag, energy[0], 0.0) - square * m66[0] + y[0]
+    )
+    ready[N : 2 * N, :] = (
+        jnp.where(diag, BROADENING, 0.0) - square * m66[1] + y[1]
+    )
     ready[2 * N : 2 * N + 8, :] = jnp.concatenate(
-        [rhs_r, rhs_i, link, bond, jnp.zeros((4, N), jnp.float32)], 0
+        [
+            p3[3:4] + c6 * t[2:3] + onto[0],
+            p3[5:6] + c6 * t[3:4] + onto[1],
+            link,
+            p3[1:2],
+            jnp.zeros((4, N), jnp.float32),
+        ],
+        0,
     )
 
 
@@ -221,34 +351,48 @@
     invert(ar, ai)
     mat[0] = ar[...]
     mat[1] = ai[...]
-    q_r, q_i = apply(side[0:1], side[1:2], ar[...], ai[...])
-    vec[...] = jnp.concatenate([q_r, q_i, side[2:8]], 0)
-
-
-def last_kernel(flag, weight, far, m0, v0, m1, v1, m7, v7, out, ar, ai):
-    all_m = [m0.at[0], m0.at[1]] + [m1.at[j] for j in range(5)]
-    all_v = [v0[0], v0[1]] + [v1[j] for j in range(5)]
+    q_r, q_i = apply((side[0:1], side[1:2]), ar[...], ai[...])
+    vec[...] = jnp.concatenate([-q_r, -q_i, side[2:8]], 0)
+
+
+def last_kernel(flag, weight, far, m0, v0, m1, v1, m4, v4, m7, v7, mid, out, ar, ai):
     side = far[2 * N : 2 * N + 8, :]
     own = v7[...]
     middle = jnp.where(flag[0] == 1, side[3:4], own[3:4])
-    scale = outer_square(middle)
+    scale = down(middle) * middle
     ar[...] = far[0:N, :] + scale * m7[0]
     ai[...] = far[N : 2 * N, :] + scale * m7[1]
-    rhs_r = side[0:1] + middle * own[0:1]
-    rhs_i = side[1:2] + middle * own[1:2]
+    rhs = (side[0:1] + middle * own[0:1], side[1:2] + middle * own[1:2])
     invert(ar, ai)
-    now_r, now_i = apply(rhs_r, rhs_i, ar[...], ai[...])
-    rows = []
-    link = middle
-    for mat, vec in [(m7, own)] + [(all_m[j], all_v[j]) for j in range(6, -1, -1)]:
-        add_r, add_i = apply(link * now_r, link * now_i, mat[0], mat[1])
-        now_r = vec[0:1] + add_r
-        now_i = vec[1:2] + add_i
-        rows.append(weight[0] * (now_r * now_r + now_i * now_i))
-        link = vec[2:3]
-    turned = flag[0] == 1
-    low, high = rows[::-1], rows
-    out[...] = jnp.where(turned, jnp.concatenate(high, 0), jnp.concatenate(low, 0))
+    v_r, v_i = apply(rhs, ar[...], ai[...])
+    psi = {8: (-v_r, -v_i)}
+    scaled = lambda c, v: (c * v[0], c * v[1])
+
+    def back(q, link, later, mat_r, mat_i):
+        add = apply(scaled(link, later), mat_r, mat_i)
+        return q[0:1] - add[0], q[1:2] - add[1]
+
+    psi[7] = back(own, middle, psi[8], m7[0], m7[1])
+    four = v4[...]
+    c4, c6 = four[3:4], four[4:5]
+    t = mid[5 * N : 5 * N + 8, :]
+    right = scaled(c6, psi[7])
+    w = apply(right, mid[0:N, :], mid[N : 2 * N, :], turned=True)
+    psi[4] = back(four, c4, w, m4[0], m4[1])
+    left = scaled(c4, psi[4])
+    a = apply(left, *unfold(mid[2 * N : 3 * N, :], t[4:5]))
+    psi[5] = (t[0:1] + a[0] + w[0], t[1:2] + a[1] + w[1])
+    b = apply(left, mid[0:N, :], mid[N : 2 * N, :])
+    c = apply(right, *unfold(mid[3 * N : 4 * N, :], t[5:6]))
+    psi[6] = (t[2:3] + b[0] + c[0], t[3:4] + b[1] + c[1])
+    psi[3] = back(v1[1], four[2:3], psi[4], m1[1, 0], m1[1, 1])
+    psi[2] = back(v1[0], v1[1, 2:3, :], psi[3], m1[0, 0], m1[0, 1])
+    psi[1] = back(v0[1], v1[0, 2:3, :], psi[2], m0[1, 0], m0[1, 1])
+    psi[0] = back(v0[0], v0[1, 2:3, :], psi[1], m0[0, 0], m0[0, 1])
+    rows = [weight[0] * (psi[j][0] * psi[j][0] + psi[j][1] * psi[j][1]) for j in range(8)]
+    out[...] = jnp.where(
+        flag[0] == 1, jnp.concatenate(rows[::-1], 0), jnp.concatenate(rows, 0)
+    )
 
 
 SMEM = pl.BlockSpec(memory_space=pltpu.SMEM)
@@ -293,38 +437,39 @@
     vecs = jnp.where(flip, vecs[:, ::-1], vecs).reshape(6, N)
     vecs = jnp.concatenate([vecs, jnp.zeros((2, N), jnp.float32)], 0)
     own = call(prep_kernel, [flag], [got, vecs], shape(PACK, N), [])
-    packs = [
-        lax.ppermute(own, "slab", [(1, 0), (6, 7)]),
-        lax.ppermute(own, "slab", [(2, 0), (5, 7)]),
-        lax.ppermute(own, "slab", [(3, 0), (4, 7)]),
-    ]
-    scalars = [flag, energies]
-    m0, v0 = call(
+    after = lax.ppermute(own, "slab", [(1, 0), (6, 7), (3, 2), (4, 5)])
+    inner = ((slab == 2) | (slab == 5)).astype(jnp.int32)[None]
+    pair = [shape(2, 2, N, N), shape(2, 8, N)]
+    square = [shape(2, N, N), shape(8, N)]
+    room = [MATRIX, MATRIX]
+    sides = pltpu.VMEM((2, 8, N), jnp.float32)
+    m0, v0, mid = call(
         first_kernel,
-        scalars,
-        [own],
-        [shape(2, 2, N, N), shape(2, 8, N)],
-        [MATRIX, MATRIX, SIDE],
+        [flag, inner, energies],
+        [own, after],
+        pair + [shape(5 * N + 24, N)],
+        room + [SIDE, pltpu.VMEM((2, N, N), jnp.float32), sides],
         2,
     )
-    m1, v1, ready = call(
-        middle_kernel,
-        scalars,
-        packs + [m0, v0],
-        [shape(5, 2, N, N), shape(5, 8, N), shape(PACK, N)],
-        [MATRIX, MATRIX, SIDE, pltpu.VMEM((6, N, N), jnp.float32), pltpu.VMEM((3, 8, N), jnp.float32)],
-        5,
+    mid = lax.ppermute(mid, "slab", [(2, 0), (5, 7)])
+    m1, v1 = call(
+        second_kernel, [flag, energies], [after, m0, v0], pair, room + [SIDE, sides], 2
+    )
+    m4, v4, ready = call(
+        third_kernel,
+        [flag, energies],
+        [m1, v1, mid],
+        square + [shape(PACK, N)],
+        room,
     )
     far = lax.ppermute(ready, "slab", [(0, 7), (7, 0)])
-    m7, v7 = call(
-        inner_kernel, [], [ready], [shape(2, N, N), shape(8, N)], [MATRIX, MATRIX]
-    )
+    m7, v7 = call(inner_kernel, [], [ready], square, room)
     density = call(
         last_kernel,
         [flag, weights],
-        [far, m0, v0, m1, v1, m7, v7],
+        [far, m0, v0, m1, v1, m4, v4, m7, v7, mid],
         shape(8, N),
-        [MATRIX, MATRIX],
+        room,
     )
     parts = density.reshape(4, 2, 16, 16)
     low = jnp.where(slab == 0, parts, 0.0)

time: 156 us -> 142 us (0.910)
  Pallas kernels: 103 us -> 86.2 us
  waiting for transfers between devices: 9.6 us -> 12.4 us
  blocking collectives: 17.1 us -> 18.7 us
    pallas_call x5 -> x6, Pallas kernels: 103 us -> 86.2 us  [call(): pl.pallas_call(kernel, out_shape=outs, in_specs=[SMEM] * len(scalars) + [...]
    all_to_all x1, waiting for transfers between devices: 9.58 us -> 11.6 us  [shards(): lax.all_to_all(jnp.broadcast_to(piece[None], (16, 40, N)), 'energy', 0, 0)]
    all_to_all x1, blocking collectives: 17.1 us -> 18.7 us  [shards(): return jnp.sum(lax.all_to_all(sent, ('slab', 'energy'), 0, 0), axis=0)]
    ppermute x3 -> x2, starting transfers between devices: 5.45 us -> 4.8 us  [the longest x1 4.06 us: shards(): after = lax.ppermute(own, 'slab', [(1, 0), (6, 7), (3, 2), (4, 5)])]
    unnamed x4 -> x12, local copies, waits for them, and re-layouts: 3.25 us -> 2.92 us
  transfers between devices with their start and end apart: 5 -> 4, of which waited for: 1 -> 2; matrix products, arithmetic and copies ran while one was open for 1% -> 0% of each run, Pallas kernels for 21% -> 24%
where the time goes in v3:
time: 142 us; the launch traced here: 141 us
  Pallas kernels  86.2 us (61%)
  blocking collectives  18.7 us (13%)
  starting transfers between devices  14.9 us (10%)
  waiting for transfers between devices  12.4 us (9%)
  local copies, waits for them, and re-layouts  5.23 us (4%)
  other arithmetic  2.48 us (2%)
  between operations  1.52 us (1%)
    pallas_call x6, Pallas kernels, call(): pl.pallas_call(kernel, out_shape=outs, in_specs=[SMEM] * len(scalars) + [...  86.2 us
    all_to_all x1, blocking collectives, shards(): return jnp.sum(lax.all_to_all(sent, ('slab', 'energy'), 0, 0), axis=0)  18.7 us
    all_to_all x1, waiting for transfers between devices, shards(): lax.all_to_all(jnp.broadcast_to(piece[None], (16, 40, N)), 'energy', 0, 0)  11.6 us
    all_to_all x1, starting transfers between devices, shards(): lax.all_to_all(jnp.broadcast_to(piece[None], (16, 40, N)), 'energy', 0, 0)  8.6 us
    ppermute x1, starting transfers between devices, shards(): after = lax.ppermute(own, 'slab', [(1, 0), (6, 7), (3, 2), (4, 5)])  4.06 us
    unnamed x12, local copies, waits for them, and re-layouts  2.92 us
  transfers between devices with their start and end apart: 4, of which 2 were waited for; matrix products, arithmetic and copies ran while one was open for 0% of the time, Pallas kernels for 24%

profile of v3, /device:TPU:1, one launch (start us, length us, event | category | flops | bytes accessed | tf_op | source)
XLA Modules:
  0.0 141.4 jit_solution(13277667390508790913)
XLA Ops:
  0.0 0.0 copy-start.5
  0.0 0.0 copy-start.4
  0.0 0.8 dynamic_slice.3
  0.8 0.1 iota_compare_fusion
  0.9 0.7 multiply_add_fusion
  1.6 0.1 select_reduce_fusion
  1.7 0.1 pad.8.clone
  1.7 0.8 maximum_maximum_fusion
  2.6 0.9 broadcast_in_dim.54
  3.5 8.6 %all-to-all-start = ((f32[16,40,256]{2,1,0:T(8,128)}), f32[16,40,256]{2,1,0:T(8,128)S(1)}, u32[]{:S(2)}, u32[]{:S(2)}) async-start(f32[16,40,256]{2,1,0:T(8,128)} %broadcast_in_dim.54), calls=%async_computation | async-start | bytes 1310720 | tf_op jit(solution)/shard_map/all_to_all | solution.py:433
  12.1 0.0 copy-done.5
  12.1 0.0 copy-done.4
  12.1 0.1 rev.3
  12.3 11.6 %all-to-all-done.got = f32[16,40,256]{2,1,0:T(8,128)S(1)} async-done(((f32[16,40,256]{2,1,0:T(8,128)}), f32[16,40,256]{2,1,0:T(8,128)S(1)}, u32[]{:S(2)}, u32[]{:S(2)}) %all-to-all-start) | async-done | bytes 655392 | tf_op jit(solution)/shard_map/all_to_all | solution.py:433
  23.8 0.2 shard_map.91.own
  24.1 4.1 %collective-permute-start = (f32[520,256]{1,0:T(8,128)S(1)}, f32[520,256]{1,0:T(8,128)S(1)}, u32[]{:S(2)}, u32[]{:S(2)}) collective-permute-start(f32[520,256]{1,0:T(8,128)S(1)} %shard_map.91.own), channel_id=1, source_target_pairs={{1,0},{6,7},{3,2},{4,5},{9,8},{14,15},{11,10},{12,13},{17,16},{22,... | collective-permute-start | bytes 1597448 | tf_op jit(solution)/shard_map/ppermute | solution.py:440
  28.8 0.8 collective-permute-done.after
  29.6 0.0 copy-start
  29.6 22.3 %shard_map.92 = (f32[2,2,256,256]{3,2,1,0:T(8,128)S(1)}, f32[2,8,256]{2,1,0:T(8,128)S(1)}, f32[1304,256]{1,0:T(8,128)S(1)}) custom-call(s32[1]{0:T(128)} %bitcast.flag, s32[1]{0:T(128)} %bitcast.5.inner, f32[1]{0:T(128)S(6)} %copy.19.energy, f32[520,256]{1,0:T(8,128)S(1)} %shard_map.91.own, f32[520,256]{1,0:T(8,128)S(1)} %collective-permute-done.after), custom_call_target="tpu_custom_call" | custom-call | flops 268435456 | bytes 524288 | tf_op jit(solution)/shard_map/pallas_call | solution.py:410
  51.9 0.0 copy-done
  51.9 0.7 collective-permute-start.1
  52.6 0.0 copy-start.1
  52.7 1.0 copy-done.1
  53.7 22.2 %shard_map.93 = (f32[2,2,256,256]{3,2,1,0:T(8,128)S(1)}, f32[2,8,256]{2,1,0:T(8,128)S(1)}) custom-call(s32[1]{0:T(128)} %bitcast.flag, f32[1]{0:T(128)S(6)} %copy.19.energy, f32[520,256]{1,0:T(8,128)S(1)} %copy-done.1, f32[2,2,256,256]{3,2,1,0:T(8,128)S(1)} %get-tuple-element.15.start.m0, f32[2,8,256]{2,1,0:T(8,128)S(1)} %get-tuple-element.16.before.v0), custom_call_target="tpu_custom_call" | custom-call | flops 268435456 | bytes 524288 | tf_op jit(solution)/shard_map/pallas_call | solution.py:410
  75.9 0.0 collective-permute-done.1.mid
  75.9 14.3 %shard_map.94 = (f32[2,256,256]{2,1,0:T(8,128)S(1)}, f32[8,256]{1,0:T(8,128)S(1)}, f32[520,256]{1,0:T(8,128)}) custom-call(s32[1]{0:T(128)} %bitcast.flag, f32[1]{0:T(128)S(6)} %copy.19.energy, f32[2,2,256,256]{3,2,1,0:T(8,128)S(1)} %get-tuple-element.17.start.m1, f32[2,8,256]{2,1,0:T(8,128)S(1)} %get-tuple-element.18.before.v1, ...), custom_call_target="tpu_custom_call" | custom-call | flops 134217728 | bytes 262144 | tf_op jit(solution)/shard_map/pallas_call | solution.py:410
  90.2 0.0 copy-start.2
  90.2 0.8 copy-done.2
  91.0 1.5 %collective-permute-start.2 = (f32[520,256]{1,0:T(8,128)}, f32[520,256]{1,0:T(8,128)}, u32[]{:S(2)}, u32[]{:S(2)}) collective-permute-start(f32[520,256]{1,0:T(8,128)} %get-tuple-element.20.ready), channel_id=1, source_target_pairs={{0,7},{7,0},{8,15},{15,8},{16,23},{23,16},{24,31},{31,24},{32,39},... | collective-permute-start | bytes 1597448 | tf_op jit(solution)/shard_map/ppermute | solution.py:465
  93.1 12.0 %shard_map.95 = (f32[2,256,256]{2,1,0:T(8,128)S(1)}, f32[8,256]{1,0:T(8,128)S(1)}) custom-call(f32[520,256]{1,0:T(8,128)} %get-tuple-element.20.ready), custom_call_target="tpu_custom_call" | custom-call | flops 134217728 | bytes 262144 | tf_op jit(solution)/shard_map/pallas_call | solution.py:410
  105.2 0.0 collective-permute-done.2.far
  105.2 0.0 copy-start.3
  105.2 1.0 copy-done.3
  106.2 15.2 %shard_map.96 = f32[8,256]{1,0:T(8,128)S(1)} custom-call(s32[1]{0:T(128)} %bitcast.flag, f32[1]{0:T(128)S(6)} %copy.20.weight, f32[520,256]{1,0:T(8,128)} %collective-permute-done.2.far, f32[2,2,256,256]{3,2,1,0:T(8,128)S(1)} %get-tuple-element.15.start.m0, f32[2,8,256]{2,1,0:T(8,128)S(1)} %get-tuple-element.16.before.v0, ...), custom_call_target="tpu_custom_call" | custom-call | flops 134217728 | bytes 262144 | tf_op jit(solution)/shard_map/pallas_call | solution.py:410
  121.4 0.1 select_n.41
  121.5 0.1 copy.15
  121.6 0.1 select_n.44
  121.7 0.1 copy.16
  121.8 0.1 copy.18
  122.0 18.7 %all_to_all.10 = f32[128,2,16]{2,1,0:T(2,128)S(1)} all-to-all(f32[128,2,16]{2,1,0:T(2,128)S(1)} %bitcast.11), channel_id=1, replica_groups=mesh['energy'=16,'slab'=8] {'slab','energy'}, dimensions={0} | all-to-all | bytes 32768 | tf_op jit(solution)/shard_map/all_to_all | solution.py:478
  140.7 0.7 reduce_sum.19
  (8 shorter events, 0.1 us)
Async XLA Ops:
  0.0 12.1 %copy-start.5 = (f32[2,1,2,256]{3,2,1,0:T(2,128)S(1)}, f32[2,1,2,256]{3,2,1,0:T(2,128)}, u32[]{:S(2)}) copy-start(f32[2,1,2,256]{3,2,1,0:T(2,128)} %param.17) | copy-start | bytes 12292
  0.0 12.1 %copy-start.4 = (f32[2,256]{1,0:T(2,128)S(1)}, f32[2,256]{1,0:T(2,128)}, u32[]{:S(2)}) copy-start(f32[2,256]{1,0:T(2,128)} %param.14) | copy-start | bytes 6148
  3.5 20.4 %all-to-all-start = ((f32[16,40,256]{2,1,0:T(8,128)}), f32[16,40,256]{2,1,0:T(8,128)S(1)}, u32[]{:S(2)}, u32[]{:S(2)}) async-start(f32[16,40,256]{2,1,0:T(8,128)} %broadcast_in_dim.54), calls=%async_computation | async-start | bytes 1310720 | tf_op jit(solution)/shard_map/all_to_all | solution.py:433
  24.1 5.6 %collective-permute-start = (f32[520,256]{1,0:T(8,128)S(1)}, f32[520,256]{1,0:T(8,128)S(1)}, u32[]{:S(2)}, u32[]{:S(2)}) collective-permute-start(f32[520,256]{1,0:T(8,128)S(1)} %shard_map.91.own), channel_id=1, source_target_pairs={{1,0},{6,7},{3,2},{4,5},{9,8},{14,15},{11,10},{12,13},{17,16},{22,... | collective-permute-start | bytes 1597448 | tf_op jit(solution)/shard_map/ppermute | solution.py:440
  29.6 22.3 %copy-start = (f32[520,256]{1,0:T(8,128)}, f32[520,256]{1,0:T(8,128)S(1)}, u32[]{:S(2)}) copy-start(f32[520,256]{1,0:T(8,128)S(1)} %collective-permute-done.after) | copy-start | bytes 1597444
  51.9 24.0 %collective-permute-start.1 = (f32[1304,256]{1,0:T(8,128)S(1)}, f32[1304,256]{1,0:T(8,128)S(1)}, u32[]{:S(2)}, u32[]{:S(2)}) collective-permute-start(f32[1304,256]{1,0:T(8,128)S(1)} %get-tuple-element.19), channel_id=1, source_target_pairs={{2,0},{5,7},{10,8},{13,15},{18,16},{21,23},{26,24},{29,31},{34,32}... | collective-permute-start | bytes 4005896 | tf_op jit(solution)/shard_map/ppermute | solution.py:454
  52.6 1.0 copy-start.1
  90.2 0.8 copy-start.2
  91.0 14.1 %collective-permute-start.2 = (f32[520,256]{1,0:T(8,128)}, f32[520,256]{1,0:T(8,128)}, u32[]{:S(2)}, u32[]{:S(2)}) collective-permute-start(f32[520,256]{1,0:T(8,128)} %get-tuple-element.20.ready), channel_id=1, source_target_pairs={{0,7},{7,0},{8,15},{15,8},{16,23},{23,16},{24,31},{31,24},{32,39},... | collective-permute-start | bytes 1597448 | tf_op jit(solution)/shard_map/ppermute | solution.py:465
  105.2 1.0 copy-start.3

commit v4 on v3

--- a/solution.py
+++ b/solution.py
@@ -144,6 +144,14 @@
 
 
 def apply(v, gr, gi, turned=False):
+    if not turned:
+        tall = [jnp.broadcast_to(x, (128, N)).T for x in v]
+        halves = [[], []]
+        for h in range(0, N, 128):
+            a, b = gr[:, h : h + 128], gi[:, h : h + 128]
+            halves[0].append(jnp.sum(tall[0] * a - tall[1] * b, axis=0, keepdims=True))
+            halves[1].append(jnp.sum(tall[0] * b + tall[1] * a, axis=0, keepdims=True))
+        return jnp.concatenate(halves[0], 1), jnp.concatenate(halves[1], 1)
     both = jnp.concatenate([v[0], v[1], jnp.zeros((6, N), jnp.float32)], 0)
     a = row_times(both, gr, turned)
     b = row_times(both, gi, turned)
@@ -219,13 +227,14 @@
     return one, two
 
 
-def first_kernel(flag, inner, energy, own, after, mats, vecs, mid, ar, ai, carry, hop, side):
+def first_kernel(flag, inner, energy, own, after, mats, vecs, mid, kept, ar, ai, carry, hop, side):
     ar[...] = jnp.zeros((N, N), jnp.float32)
     ai[...] = jnp.zeros((N, N), jnp.float32)
     carry[...] = jnp.zeros((8, N), jnp.float32)
     first = own[2 * N : 2 * N + 8, :]
     second = after[2 * N : 2 * N + 8, :]
     is_inner = inner[0] == 1
+    kept[...] = after[...]
     hop[0] = jnp.where(is_inner, own[N : 2 * N, :], own[0:N, :])
     hop[1] = jnp.where(is_inner, after[0:N, :], own[N : 2 * N, :])
     rows = lambda m, b: jnp.concatenate([m[b : b + 1], m[2 + b : 3 + b], m[4 + b : 5 + b]] * 2, 0)
@@ -344,9 +353,10 @@
     )
 
 
-def inner_kernel(ready, mat, vec, ar, ai):
+def inner_kernel(ready, four, mat, vec, held, ar, ai):
     ar[...] = ready[0:N, :]
     ai[...] = ready[N : 2 * N, :]
+    held[...] = four[...]
     side = ready[2 * N : 2 * N + 8, :]
     invert(ar, ai)
     mat[0] = ar[...]
@@ -443,17 +453,17 @@
     square = [shape(2, N, N), shape(8, N)]
     room = [MATRIX, MATRIX]
     sides = pltpu.VMEM((2, 8, N), jnp.float32)
-    m0, v0, mid = call(
+    m0, v0, mid, kept = call(
         first_kernel,
         [flag, inner, energies],
         [own, after],
-        pair + [shape(5 * N + 24, N)],
+        pair + [shape(5 * N + 24, N), shape(PACK, N)],
         room + [SIDE, pltpu.VMEM((2, N, N), jnp.float32), sides],
         2,
     )
     mid = lax.ppermute(mid, "slab", [(2, 0), (5, 7)])
     m1, v1 = call(
-        second_kernel, [flag, energies], [after, m0, v0], pair, room + [SIDE, sides], 2
+        second_kernel, [flag, energies], [kept, m0, v0], pair, room + [SIDE, sides], 2
     )
     m4, v4, ready = call(
         third_kernel,
@@ -463,7 +473,7 @@
         room,
     )
     far = lax.ppermute(ready, "slab", [(0, 7), (7, 0)])
-    m7, v7 = call(inner_kernel, [], [ready], square, room)
+    m7, v7, m4 = call(inner_kernel, [], [ready, m4], square + [shape(2, N, N)], room)
     density = call(
         last_kernel,
         [flag, weights],

time: 142 us -> 137 us (0.965)
  Pallas kernels: 86.2 us -> 83.2 us
    pallas_call x6, Pallas kernels: 86.2 us -> 83.2 us  [call(): pl.pallas_call(kernel, out_shape=outs, in_specs=[SMEM] * len(scalars) + [...]
    unnamed x12 -> x8, local copies, waits for them, and re-layouts: 2.92 us -> 1.86 us
  transfers between devices with their start and end apart: 4 -> 4, of which waited for: 2 -> 2; matrix products, arithmetic and copies ran while one was open for 0% -> 0% of each run, Pallas kernels for 24% -> 25%
where the time goes in v4:
time: 137 us
  Pallas kernels  83.2 us (61%)
  blocking collectives  17.9 us (13%)
  starting transfers between devices  14.9 us (11%)
  waiting for transfers between devices  12.4 us (9%)
  local copies, waits for them, and re-layouts  4.16 us (3%)
  other arithmetic  2.48 us (2%)
  between operations  1.52 us (1%)
    pallas_call x6, Pallas kernels, call(): pl.pallas_call(kernel, out_shape=outs, in_specs=[SMEM] * len(scalars) + [...  83.2 us
    all_to_all x1, blocking collectives, shards(): return jnp.sum(lax.all_to_all(sent, ('slab', 'energy'), 0, 0), axis=0)  17.9 us
    all_to_all x1, waiting for transfers between devices, shards(): lax.all_to_all(jnp.broadcast_to(piece[None], (16, 40, N)), 'energy', 0, 0)  11.6 us
    all_to_all x1, starting transfers between devices, shards(): lax.all_to_all(jnp.broadcast_to(piece[None], (16, 40, N)), 'energy', 0, 0)  8.6 us
    ppermute x1, starting transfers between devices, shards(): after = lax.ppermute(own, 'slab', [(1, 0), (6, 7), (3, 2), (4, 5)])  4.06 us
  transfers between devices with their start and end apart: 4, of which 2 were waited for; matrix products, arithmetic and copies ran while one was open for 0% of the time, Pallas kernels for 25%

profile of v4, /device:TPU:1, one launch (start us, length us, event | category | flops | bytes accessed | tf_op | source)
XLA Modules:
  0.0 136.6 jit_solution(14641605381952128335)
XLA Ops:
  0.0 0.0 copy-start.3
  0.0 0.0 copy-start.2
  0.0 0.8 dynamic_slice.3
  0.8 0.1 iota_compare_fusion
  0.9 0.7 multiply_add_fusion
  1.6 0.1 select_reduce_fusion
  1.7 0.1 pad.8.clone
  1.7 0.8 maximum_maximum_fusion
  2.6 0.9 broadcast_in_dim.56
  3.5 8.6 %all-to-all-start = ((f32[16,40,256]{2,1,0:T(8,128)}), f32[16,40,256]{2,1,0:T(8,128)S(1)}, u32[]{:S(2)}, u32[]{:S(2)}) async-start(f32[16,40,256]{2,1,0:T(8,128)} %broadcast_in_dim.56), calls=%async_computation | async-start | bytes 1310720 | tf_op jit(solution)/shard_map/all_to_all | solution.py:443
  12.1 0.0 copy-done.3
  12.1 0.0 copy-done.2
  12.1 0.1 rev.3
  12.3 11.6 %all-to-all-done.got = f32[16,40,256]{2,1,0:T(8,128)S(1)} async-done(((f32[16,40,256]{2,1,0:T(8,128)}), f32[16,40,256]{2,1,0:T(8,128)S(1)}, u32[]{:S(2)}, u32[]{:S(2)}) %all-to-all-start) | async-done | bytes 655392 | tf_op jit(solution)/shard_map/all_to_all | solution.py:443
  23.8 0.2 shard_map.91.own
  24.0 4.1 %collective-permute-start = (f32[520,256]{1,0:T(8,128)S(1)}, f32[520,256]{1,0:T(8,128)S(1)}, u32[]{:S(2)}, u32[]{:S(2)}) collective-permute-start(f32[520,256]{1,0:T(8,128)S(1)} %shard_map.91.own), channel_id=1, source_target_pairs={{1,0},{6,7},{3,2},{4,5},{9,8},{14,15},{11,10},{12,13},{17,16},{22,... | collective-permute-start | bytes 1597448 | tf_op jit(solution)/shard_map/ppermute | solution.py:450
  28.8 0.8 collective-permute-done.after
  29.6 21.9 %shard_map.92 = (f32[2,2,256,256]{3,2,1,0:T(8,128)S(1)}, f32[2,8,256]{2,1,0:T(8,128)S(1)}, f32[1304,256]{1,0:T(8,128)S(1)}, f32[520,256]{1,0:T(8,128)S(1)}) custom-call(s32[1]{0:T(128)} %bitcast.flag, s32[1]{0:T(128)} %bitcast.1.inner, f32[1]{0:T(128)S(6)} %copy.19.energy, f32[520,256]{1,0:T(8,128)S(1)} %shard_map.91.own, ...), custom_call_target="tpu_custom_call" | custom-call | flops 268435456 | bytes 524288 | tf_op jit(solution)/shard_map/pallas_call | solution.py:420
  51.5 0.7 collective-permute-start.1
  52.2 21.8 %shard_map.93 = (f32[2,2,256,256]{3,2,1,0:T(8,128)S(1)}, f32[2,8,256]{2,1,0:T(8,128)S(1)}) custom-call(s32[1]{0:T(128)} %bitcast.flag, f32[1]{0:T(128)S(6)} %copy.19.energy, f32[520,256]{1,0:T(8,128)S(1)} %get-tuple-element.17.after, f32[2,2,256,256]{3,2,1,0:T(8,128)S(1)} %get-tuple-element.18.start.m0, f32[2,8,256]{2,1,0:T(8,128)S(1)} %get-tuple-element.19.before.v0), custom_call_target="tpu_custom_call" | custom-call | flops 268435456 | bytes 524288 | tf_op jit(solution)/shard_map/pallas_call | solution.py:420
  74.0 0.0 collective-permute-done.1.mid
  74.0 13.9 %shard_map.94 = (f32[2,256,256]{2,1,0:T(8,128)S(1)}, f32[8,256]{1,0:T(8,128)S(1)}, f32[520,256]{1,0:T(8,128)}) custom-call(s32[1]{0:T(128)} %bitcast.flag, f32[1]{0:T(128)S(6)} %copy.19.energy, f32[2,2,256,256]{3,2,1,0:T(8,128)S(1)} %get-tuple-element.20.start.m1, f32[2,8,256]{2,1,0:T(8,128)S(1)} %get-tuple-element.21.before.v1, ...), custom_call_target="tpu_custom_call" | custom-call | flops 134217728 | bytes 262144 | tf_op jit(solution)/shard_map/pallas_call | solution.py:420
  88.0 0.0 copy-start
  88.0 0.8 copy-done
  88.8 1.5 %collective-permute-start.2 = (f32[520,256]{1,0:T(8,128)}, f32[520,256]{1,0:T(8,128)}, u32[]{:S(2)}, u32[]{:S(2)}) collective-permute-start(f32[520,256]{1,0:T(8,128)} %get-tuple-element.23.ready), channel_id=1, source_target_pairs={{0,7},{7,0},{8,15},{15,8},{16,23},{23,16},{24,31},{31,24},{32,39},... | collective-permute-start | bytes 1597448 | tf_op jit(solution)/shard_map/ppermute | solution.py:475
  90.9 0.0 copy-start.1
  90.9 1.0 copy-done.1
  91.9 11.8 %shard_map.95 = (f32[2,256,256]{2,1,0:T(8,128)S(1)}, f32[8,256]{1,0:T(8,128)S(1)}, f32[2,256,256]{2,1,0:T(8,128)S(1)}) custom-call(f32[520,256]{1,0:T(8,128)} %get-tuple-element.23.ready, f32[2,256,256]{2,1,0:T(8,128)S(1)} %copy-done.1), custom_call_target="tpu_custom_call" | custom-call | flops 134217728 | bytes 262144 | tf_op jit(solution)/shard_map/pallas_call | solution.py:420
  103.8 0.0 collective-permute-done.2.far
  103.8 13.6 %shard_map.96 = f32[8,256]{1,0:T(8,128)S(1)} custom-call(s32[1]{0:T(128)} %bitcast.flag, f32[1]{0:T(128)S(6)} %copy.20.weight, f32[520,256]{1,0:T(8,128)} %collective-permute-done.2.far, f32[2,2,256,256]{3,2,1,0:T(8,128)S(1)} %get-tuple-element.18.start.m0, f32[2,8,256]{2,1,0:T(8,128)S(1)} %get-tuple-element.19.before.v0, ...), custom_call_target="tpu_custom_call" | custom-call | flops 134217728 | bytes 262144 | tf_op jit(solution)/shard_map/pallas_call | solution.py:420
  117.4 0.1 select_n.41
  117.5 0.1 copy.15
  117.6 0.1 select_n.44
  117.6 0.1 copy.16
  117.8 0.1 copy.18
  117.9 17.9 %all_to_all.10 = f32[128,2,16]{2,1,0:T(2,128)S(1)} all-to-all(f32[128,2,16]{2,1,0:T(2,128)S(1)} %bitcast.11), channel_id=1, replica_groups=mesh['energy'=16,'slab'=8] {'slab','energy'}, dimensions={0} | all-to-all | bytes 32768 | tf_op jit(solution)/shard_map/all_to_all | solution.py:488
  135.9 0.7 reduce_sum.19
  (8 shorter events, 0.1 us)
Async XLA Ops:
  0.0 12.1 %copy-start.3 = (f32[2,1,2,256]{3,2,1,0:T(2,128)S(1)}, f32[2,1,2,256]{3,2,1,0:T(2,128)}, u32[]{:S(2)}) copy-start(f32[2,1,2,256]{3,2,1,0:T(2,128)} %param.17) | copy-start | bytes 12292
  0.0 12.1 %copy-start.2 = (f32[2,256]{1,0:T(2,128)S(1)}, f32[2,256]{1,0:T(2,128)}, u32[]{:S(2)}) copy-start(f32[2,256]{1,0:T(2,128)} %param.14) | copy-start | bytes 6148
  3.5 20.4 %all-to-all-start = ((f32[16,40,256]{2,1,0:T(8,128)}), f32[16,40,256]{2,1,0:T(8,128)S(1)}, u32[]{:S(2)}, u32[]{:S(2)}) async-start(f32[16,40,256]{2,1,0:T(8,128)} %broadcast_in_dim.56), calls=%async_computation | async-start | bytes 1310720 | tf_op jit(solution)/shard_map/all_to_all | solution.py:443
  24.0 5.6 %collective-permute-start = (f32[520,256]{1,0:T(8,128)S(1)}, f32[520,256]{1,0:T(8,128)S(1)}, u32[]{:S(2)}, u32[]{:S(2)}) collective-permute-start(f32[520,256]{1,0:T(8,128)S(1)} %shard_map.91.own), channel_id=1, source_target_pairs={{1,0},{6,7},{3,2},{4,5},{9,8},{14,15},{11,10},{12,13},{17,16},{22,... | collective-permute-start | bytes 1597448 | tf_op jit(solution)/shard_map/ppermute | solution.py:450
  51.5 22.6 %collective-permute-start.1 = (f32[1304,256]{1,0:T(8,128)S(1)}, f32[1304,256]{1,0:T(8,128)S(1)}, u32[]{:S(2)}, u32[]{:S(2)}) collective-permute-start(f32[1304,256]{1,0:T(8,128)S(1)} %get-tuple-element.22), channel_id=1, source_target_pairs={{2,0},{5,7},{10,8},{13,15},{18,16},{21,23},{26,24},{29,31},{34,32}... | collective-permute-start | bytes 4005896 | tf_op jit(solution)/shard_map/ppermute | solution.py:464
  88.0 0.8 copy-start
  88.8 15.0 %collective-permute-start.2 = (f32[520,256]{1,0:T(8,128)}, f32[520,256]{1,0:T(8,128)}, u32[]{:S(2)}, u32[]{:S(2)}) collective-permute-start(f32[520,256]{1,0:T(8,128)} %get-tuple-element.23.ready), channel_id=1, source_target_pairs={{0,7},{7,0},{8,15},{15,8},{16,23},{23,16},{24,31},{31,24},{32,39},... | collective-permute-start | bytes 1597448 | tf_op jit(solution)/shard_map/ppermute | solution.py:475
  90.9 1.0 copy-start.1

commit v5 on v4

--- a/solution.py
+++ b/solution.py
@@ -227,26 +227,39 @@
     return one, two
 
 
-def first_kernel(flag, inner, energy, own, after, mats, vecs, mid, kept, ar, ai, carry, hop, side):
+def rows_of(pack, b):
+    side = pack[2 * N : 2 * N + 8, :]
+    return jnp.concatenate([side[b : b + 1], side[2 + b : 3 + b], side[4 + b : 5 + b]], 0)
+
+
+def start_kernel(flag, inner, energy, own, mats, vecs, ar, ai, carry):
     ar[...] = jnp.zeros((N, N), jnp.float32)
     ai[...] = jnp.zeros((N, N), jnp.float32)
     carry[...] = jnp.zeros((8, N), jnp.float32)
+    is_inner = inner[0] == 1
+    real = jnp.where(is_inner, own[N : 2 * N, :], own[0:N, :])
+    here = jnp.where(is_inner, rows_of(own, 1), rows_of(own, 0))
+    eliminate(flag, energy, here[0:1], (here[1:2], here[2:3]), real, ar, ai, carry, mats, vecs, 0)
+
+
+def first_kernel(
+    flag, inner, energy, own, after, old, before, mats, vecs, mid, kept, ar, ai, carry, side
+):
+    ar[...] = old[0, 0]
+    ai[...] = old[0, 1]
+    carry[...] = before[0]
     first = own[2 * N : 2 * N + 8, :]
     second = after[2 * N : 2 * N + 8, :]
     is_inner = inner[0] == 1
     kept[...] = after[...]
-    hop[0] = jnp.where(is_inner, own[N : 2 * N, :], own[0:N, :])
-    hop[1] = jnp.where(is_inner, after[0:N, :], own[N : 2 * N, :])
-    rows = lambda m, b: jnp.concatenate([m[b : b + 1], m[2 + b : 3 + b], m[4 + b : 5 + b]] * 2, 0)
-    side[0, 0:6] = jnp.where(is_inner, rows(first, 1), rows(first, 0))
-    side[1, 0:6] = jnp.where(is_inner, rows(second, 0), rows(first, 1))
-
-    @pl.loop(0, 2)
-    def _(b):
-        here = side[b]
-        eliminate(
-            flag, energy, here[0:1], (here[1:2], here[2:3]), hop[b], ar, ai, carry, mats, vecs, b
-        )
+    real = jnp.where(is_inner, after[0:N, :], own[N : 2 * N, :])
+    side[0, 0:3] = rows_of(own, 1)
+    side[1, 0:3] = jnp.where(is_inner, rows_of(after, 0), rows_of(own, 1))
+    here = side[1]
+    mats[0, 0] = old[0, 0]
+    mats[0, 1] = old[0, 1]
+    vecs[0] = before[0]
+    eliminate(flag, energy, here[0:1], (here[1:2], here[2:3]), real, ar, ai, carry, mats, vecs, 1)
 
     @pl.when(is_inner)
     def _():
@@ -407,7 +420,7 @@
 
 SMEM = pl.BlockSpec(memory_space=pltpu.SMEM)
 VMEM = pl.BlockSpec(memory_space=pltpu.VMEM)
-PARAMS = pltpu.CompilerParams(vmem_limit_bytes=48 * 2**20)
+PARAMS = pltpu.CompilerParams(vmem_limit_bytes=16 * 2**20)
 MATRIX = pltpu.VMEM((N, N), jnp.float32)
 SIDE = pltpu.VMEM((8, N), jnp.float32)
 
@@ -453,13 +466,19 @@
     square = [shape(2, N, N), shape(8, N)]
     room = [MATRIX, MATRIX]
     sides = pltpu.VMEM((2, 8, N), jnp.float32)
+    old, before = call(
+        start_kernel,
+        [flag, inner, energies],
+        [own],
+        [shape(1, 2, N, N), shape(1, 8, N)],
+        room + [SIDE],
+    )
     m0, v0, mid, kept = call(
         first_kernel,
         [flag, inner, energies],
-        [own, after],
+        [own, after, old, before],
         pair + [shape(5 * N + 24, N), shape(PACK, N)],
-        room + [SIDE, pltpu.VMEM((2, N, N), jnp.float32), sides],
-        2,
+        room + [SIDE, sides],
     )
     mid = lax.ppermute(mid, "slab", [(2, 0), (5, 7)])
     m1, v1 = call(

time: 137 us -> 135 us (0.985)
    pallas_call x6 -> x7, Pallas kernels: 83.2 us -> 83.1 us  [call(): pl.pallas_call(kernel, out_shape=outs, in_specs=[SMEM] * len(scalars) + [...]
  transfers between devices with their start and end apart: 4 -> 4, of which waited for: 2 -> 1; matrix products, arithmetic and copies ran while one was open for 0% -> 0% of each run, Pallas kernels for 25% -> 33%
where the time goes in v5:
time: 135 us
  Pallas kernels  83.1 us (62%)
  blocking collectives  16.9 us (13%)
  starting transfers between devices  14.9 us (11%)
  waiting for transfers between devices  11.6 us (9%)
  local copies, waits for them, and re-layouts  4.17 us (3%)
  other arithmetic  2.48 us (2%)
  between operations  1.54 us (1%)
    pallas_call x7, Pallas kernels, call(): pl.pallas_call(kernel, out_shape=outs, in_specs=[SMEM] * len(scalars) + [...  83.1 us
    all_to_all x1, blocking collectives, shards(): return jnp.sum(lax.all_to_all(sent, ('slab', 'energy'), 0, 0), axis=0)  16.9 us
    all_to_all x1, waiting for transfers between devices, shards(): lax.all_to_all(jnp.broadcast_to(piece[None], (16, 40, N)), 'energy', 0, 0)  11.6 us
    all_to_all x1, starting transfers between devices, shards(): lax.all_to_all(jnp.broadcast_to(piece[None], (16, 40, N)), 'energy', 0, 0)  8.6 us
    ppermute x1, starting transfers between devices, shards(): after = lax.ppermute(own, 'slab', [(1, 0), (6, 7), (3, 2), (4, 5)])  4.06 us
  transfers between devices with their start and end apart: 4, of which 1 were waited for; matrix products, arithmetic and copies ran while one was open for 0% of the time, Pallas kernels for 33%

profile of v5, /device:TPU:1, one launch (start us, length us, event | category | flops | bytes accessed | tf_op | source)
XLA Modules:
  0.0 134.6 jit_solution(7242197349025510325)
XLA Ops:
  0.0 0.0 copy-start.3
  0.0 0.0 copy-start.2
  0.0 0.8 dynamic_slice.3
  0.8 0.1 iota_compare_fusion
  0.9 0.7 multiply_add_fusion
  1.6 0.1 select_reduce_fusion
  1.7 0.1 pad.8.clone
  1.7 0.8 maximum_maximum_fusion
  2.6 0.9 broadcast_in_dim.56
  3.5 8.6 %all-to-all-start = ((f32[16,40,256]{2,1,0:T(8,128)}), f32[16,40,256]{2,1,0:T(8,128)S(1)}, u32[]{:S(2)}, u32[]{:S(2)}) async-start(f32[16,40,256]{2,1,0:T(8,128)} %broadcast_in_dim.56), calls=%async_computation | async-start | bytes 1310720 | tf_op jit(solution)/shard_map/all_to_all | solution.py:456
  12.1 0.0 copy-done.3
  12.1 0.0 copy-done.2
  12.1 0.1 rev.3
  12.3 11.6 %all-to-all-done.got = f32[16,40,256]{2,1,0:T(8,128)S(1)} async-done(((f32[16,40,256]{2,1,0:T(8,128)}), f32[16,40,256]{2,1,0:T(8,128)S(1)}, u32[]{:S(2)}, u32[]{:S(2)}) %all-to-all-start) | async-done | bytes 655392 | tf_op jit(solution)/shard_map/all_to_all | solution.py:456
  23.8 0.2 shard_map.91.own
  24.1 4.1 %collective-permute-start = (f32[520,256]{1,0:T(8,128)S(1)}, f32[520,256]{1,0:T(8,128)S(1)}, u32[]{:S(2)}, u32[]{:S(2)}) collective-permute-start(f32[520,256]{1,0:T(8,128)S(1)} %shard_map.91.own), channel_id=1, source_target_pairs={{1,0},{6,7},{3,2},{4,5},{9,8},{14,15},{11,10},{12,13},{17,16},{22,... | collective-permute-start | bytes 1597448 | tf_op jit(solution)/shard_map/ppermute | solution.py:463
  28.8 10.8 %shard_map.92 = (f32[1,2,256,256]{3,2,1,0:T(8,128)S(1)}, f32[1,8,256]{2,1,0:T(8,128)S(1)}) custom-call(s32[1]{0:T(128)} %bitcast.flag, s32[1]{0:T(128)} %bitcast.1.inner, f32[1]{0:T(128)S(6)} %copy.19.energy, f32[520,256]{1,0:T(8,128)S(1)} %shard_map.91.own), custom_call_target="tpu_custom_call" | custom-call | flops 134217728 | bytes 262144 | tf_op jit(solution)/shard_map/pallas_call | solution.py:433
  39.6 0.0 collective-permute-done.after
  39.6 10.9 %shard_map.93 = (f32[2,2,256,256]{3,2,1,0:T(8,128)S(1)}, f32[2,8,256]{2,1,0:T(8,128)S(1)}, f32[1304,256]{1,0:T(8,128)S(1)}, f32[520,256]{1,0:T(8,128)S(1)}) custom-call(s32[1]{0:T(128)} %bitcast.flag, s32[1]{0:T(128)} %bitcast.1.inner, f32[1]{0:T(128)S(6)} %copy.19.energy, f32[520,256]{1,0:T(8,128)S(1)} %shard_map.91.own, ...), custom_call_target="tpu_custom_call" | custom-call | flops 134217728 | bytes 262144 | tf_op jit(solution)/shard_map/pallas_call | solution.py:433
  50.5 0.7 collective-permute-start.1
  51.3 21.8 %shard_map.94 = (f32[2,2,256,256]{3,2,1,0:T(8,128)S(1)}, f32[2,8,256]{2,1,0:T(8,128)S(1)}) custom-call(s32[1]{0:T(128)} %bitcast.flag, f32[1]{0:T(128)S(6)} %copy.19.energy, f32[520,256]{1,0:T(8,128)S(1)} %get-tuple-element.21.after, f32[2,2,256,256]{3,2,1,0:T(8,128)S(1)} %get-tuple-element.22.start.m0, f32[2,8,256]{2,1,0:T(8,128)S(1)} %get-tuple-element.23.before.v0), custom_call_target="tpu_custom_call" | custom-call | flops 268435456 | bytes 524288 | tf_op jit(solution)/shard_map/pallas_call | solution.py:433
  73.1 0.0 collective-permute-done.1.mid
  73.1 13.9 %shard_map.95 = (f32[2,256,256]{2,1,0:T(8,128)S(1)}, f32[8,256]{1,0:T(8,128)S(1)}, f32[520,256]{1,0:T(8,128)}) custom-call(s32[1]{0:T(128)} %bitcast.flag, f32[1]{0:T(128)S(6)} %copy.19.energy, f32[2,2,256,256]{3,2,1,0:T(8,128)S(1)} %get-tuple-element.24.start.m1, f32[2,8,256]{2,1,0:T(8,128)S(1)} %get-tuple-element.25.before.v1, ...), custom_call_target="tpu_custom_call" | custom-call | flops 134217728 | bytes 262144 | tf_op jit(solution)/shard_map/pallas_call | solution.py:433
  87.0 0.0 copy-start
  87.0 0.8 copy-done
  87.8 1.5 %collective-permute-start.2 = (f32[520,256]{1,0:T(8,128)}, f32[520,256]{1,0:T(8,128)}, u32[]{:S(2)}, u32[]{:S(2)}) collective-permute-start(f32[520,256]{1,0:T(8,128)} %get-tuple-element.27.ready), channel_id=1, source_target_pairs={{0,7},{7,0},{8,15},{15,8},{16,23},{23,16},{24,31},{31,24},{32,39},... | collective-permute-start | bytes 1597448 | tf_op jit(solution)/shard_map/ppermute | solution.py:494
  89.9 0.0 copy-start.1
  90.0 1.0 copy-done.1
  91.0 11.8 %shard_map.96 = (f32[2,256,256]{2,1,0:T(8,128)S(1)}, f32[8,256]{1,0:T(8,128)S(1)}, f32[2,256,256]{2,1,0:T(8,128)S(1)}) custom-call(f32[520,256]{1,0:T(8,128)} %get-tuple-element.27.ready, f32[2,256,256]{2,1,0:T(8,128)S(1)} %copy-done.1), custom_call_target="tpu_custom_call" | custom-call | flops 134217728 | bytes 262144 | tf_op jit(solution)/shard_map/pallas_call | solution.py:433
  102.8 0.0 collective-permute-done.2.far
  102.8 13.6 %shard_map.97 = f32[8,256]{1,0:T(8,128)S(1)} custom-call(s32[1]{0:T(128)} %bitcast.flag, f32[1]{0:T(128)S(6)} %copy.20.weight, f32[520,256]{1,0:T(8,128)} %collective-permute-done.2.far, f32[2,2,256,256]{3,2,1,0:T(8,128)S(1)} %get-tuple-element.22.start.m0, f32[2,8,256]{2,1,0:T(8,128)S(1)} %get-tuple-element.23.before.v0, ...), custom_call_target="tpu_custom_call" | custom-call | flops 134217728 | bytes 262144 | tf_op jit(solution)/shard_map/pallas_call | solution.py:433
  116.4 0.1 select_n.41
  116.5 0.1 copy.15
  116.6 0.1 select_n.44
  116.7 0.1 copy.16
  116.8 0.1 copy.18
  117.0 16.9 %all_to_all.10 = f32[128,2,16]{2,1,0:T(2,128)S(1)} all-to-all(f32[128,2,16]{2,1,0:T(2,128)S(1)} %bitcast.11), channel_id=1, replica_groups=mesh['energy'=16,'slab'=8] {'slab','energy'}, dimensions={0} | all-to-all | bytes 32768 | tf_op jit(solution)/shard_map/all_to_all | solution.py:507
  133.9 0.7 reduce_sum.19
  (8 shorter events, 0.1 us)
Async XLA Ops:
  0.0 12.1 %copy-start.3 = (f32[2,1,2,256]{3,2,1,0:T(2,128)S(1)}, f32[2,1,2,256]{3,2,1,0:T(2,128)}, u32[]{:S(2)}) copy-start(f32[2,1,2,256]{3,2,1,0:T(2,128)} %param.17) | copy-start | bytes 12292
  0.0 12.1 %copy-start.2 = (f32[2,256]{1,0:T(2,128)S(1)}, f32[2,256]{1,0:T(2,128)}, u32[]{:S(2)}) copy-start(f32[2,256]{1,0:T(2,128)} %param.14) | copy-start | bytes 6148
  3.5 20.4 %all-to-all-start = ((f32[16,40,256]{2,1,0:T(8,128)}), f32[16,40,256]{2,1,0:T(8,128)S(1)}, u32[]{:S(2)}, u32[]{:S(2)}) async-start(f32[16,40,256]{2,1,0:T(8,128)} %broadcast_in_dim.56), calls=%async_computation | async-start | bytes 1310720 | tf_op jit(solution)/shard_map/all_to_all | solution.py:456
  24.1 15.6 %collective-permute-start = (f32[520,256]{1,0:T(8,128)S(1)}, f32[520,256]{1,0:T(8,128)S(1)}, u32[]{:S(2)}, u32[]{:S(2)}) collective-permute-start(f32[520,256]{1,0:T(8,128)S(1)} %shard_map.91.own), channel_id=1, source_target_pairs={{1,0},{6,7},{3,2},{4,5},{9,8},{14,15},{11,10},{12,13},{17,16},{22,... | collective-permute-start | bytes 1597448 | tf_op jit(solution)/shard_map/ppermute | solution.py:463
  50.5 22.6 %collective-permute-start.1 = (f32[1304,256]{1,0:T(8,128)S(1)}, f32[1304,256]{1,0:T(8,128)S(1)}, u32[]{:S(2)}, u32[]{:S(2)}) collective-permute-start(f32[1304,256]{1,0:T(8,128)S(1)} %get-tuple-element.26), channel_id=1, source_target_pairs={{2,0},{5,7},{10,8},{13,15},{18,16},{21,23},{26,24},{29,31},{34,32}... | collective-permute-start | bytes 4005896 | tf_op jit(solution)/shard_map/ppermute | solution.py:483
  87.0 0.8 copy-start
  87.8 15.0 %collective-permute-start.2 = (f32[520,256]{1,0:T(8,128)}, f32[520,256]{1,0:T(8,128)}, u32[]{:S(2)}, u32[]{:S(2)}) collective-permute-start(f32[520,256]{1,0:T(8,128)} %get-tuple-element.27.ready), channel_id=1, source_target_pairs={{0,7},{7,0},{8,15},{15,8},{16,23},{23,16},{24,31},{31,24},{32,39},... | collective-permute-start | bytes 1597448 | tf_op jit(solution)/shard_map/ppermute | solution.py:494
  89.9 1.0 copy-start.1

commit v6 on v5

--- a/solution.py
+++ b/solution.py
@@ -23,18 +23,18 @@
 def times(x,y): return (x[0]*y[0]-x[1]*y[1],x[0]*y[1]+x[1]*y[0])
 def less(x,a,b): return (x[0]-(a[0]*b[0]-a[1]*b[1]),x[1]-(a[0]*b[1]+a[1]*b[0]))
 def row2(x,j): return (row(x[0],j),row(x[1],j))
-def panel(T,place,sub,lane):
-    half=place//128; off=place-128*half
+def panel(T,place,half,sub,lane):
+    off=place-128*half
     nt=W//8
     Z=[]
     for s in range(nt):
-        pick=lambda t: tuple(jnp.where(half==0,T[t][0][c],T[t][1][c]) for c in (0,1))
+        pick=lambda t: T[t][half]
         idx=[jnp.full(S8,off+8*s+j,jnp.int32) for j in range(8)]
         wide=lambda x: [tuple(lane_of(c,idx[j]) for c in x) for j in range(8)]
         C=wide(pick(s))
         O={t:wide(pick(t)) for t in range(s+1,nt)}
         first=place+8*s
-        for h in range(2):
+        for h in (half,):
             local=lane-(first-128*h)
             inside=(local>=0)&(local<8)
             minus=jnp.where(local==sub,-1.0,0.0)
@@ -87,7 +87,7 @@
                     for j in range(8): x=less(x,O[t][j],rows[h][j])
                     T[t][h]=x
     for t in range(nt-1):
-        for h in range(2):
+        for h in (half,):
             local=lane-(place-128*h)
             above=(local>=8*t+8)&(local<W)
             T[t][h]=tuple(jnp.where(above,0.0,x) for x in T[t][h])
@@ -96,12 +96,13 @@
 PR=((0,0),(0,1),(1,0),(1,1),(0,2),(2,0))
 def invert(ar,ai):
     sub=lax.broadcasted_iota(jnp.int32,S8,0); lane=lax.broadcasted_iota(jnp.int32,S8,1)
-    @pl.loop(0,N//W)
-    def _(k):
-        place=pl.multiple_of(k*W,W)
+    for half in (0,1):
+      @pl.loop(0,128//W)
+      def _(k):
+        place=pl.multiple_of(k*W+128*half,W)
         old=[ar[pl.ds(place,W),:],ai[pl.ds(place,W),:]]
         T=[[tuple(old[c][8*t:8*t+8,128*h:128*h+128] for c in (0,1)) for h in (0,1)] for t in range(W//8)]
-        Y,Z=panel(T,place,sub,lane)
+        Y,Z=panel(T,place,half,sub,lane)
         whole=lambda M: [jnp.concatenate([jnp.concatenate([m[0][c],m[1][c]],1) for m in M],0) for c in (0,1)]
         ys=[split3(u) for u in whole(Y)]; zs=[split3(v) for v in whole(Z)]; ns=[-v for v in zs[1]]
         left=jnp.concatenate([ys[0][a] for a,_ in PR]+[ys[1][a] for a,_ in PR],0)
@@ -109,12 +110,16 @@
         im=jnp.concatenate([zs[1][b] for _,b in PR]+[zs[0][b] for _,b in PR],0)
         right=jnp.concatenate([re,im],1)
         out=lax.dot_general(left,right,(((0,),(0,)),((),())),preferred_element_type=jnp.float32)
-        full=lax.broadcasted_iota(jnp.int32,(1,N),1)-place
-        keep=jnp.broadcast_to((full<0)|(full>=W),(N,N))
-        ar[pl.ds(place,W),:]=jnp.zeros((W,N),jnp.float32)
-        ai[pl.ds(place,W),:]=jnp.zeros((W,N),jnp.float32)
-        ar[...]=jnp.where(keep,ar[...],0.0)-out[:,:N]
-        ai[...]=jnp.where(keep,ai[...],0.0)-out[:,N:]
+        spot=place-128*half
+        full=lax.broadcasted_iota(jnp.int32,(1,128),1)
+        keep=jnp.broadcast_to((full<spot)|(full>=spot+W),(N,128))
+        for ref,at in ((ar,0),(ai,N)):
+            ref[pl.ds(place,W),:]=jnp.zeros((W,N),jnp.float32)
+            for h in (0,1):
+                lanes=slice(128*h,128*h+128)
+                was=ref[:,lanes]
+                if h==half: was=jnp.where(keep,was,0.0)
+                ref[:,lanes]=was-out[:,at+128*h:at+128*h+128]
 
 
 def prep_kernel(flag, got, vecs, out):
@@ -503,8 +508,8 @@
     parts = density.reshape(4, 2, 16, 16)
     low = jnp.where(slab == 0, parts, 0.0)
     high = jnp.where(slab == 7, parts, 0.0)
-    sent = jnp.concatenate([low, high], 0).transpose(0, 2, 1, 3).reshape(128, 2, 16)
-    return jnp.sum(lax.all_to_all(sent, ("slab", "energy"), 0, 0), axis=0)
+    sent = jnp.concatenate([low, high], 0).transpose(0, 2, 1, 3).reshape(128, 1, 32)
+    return jnp.sum(lax.all_to_all(sent, ("slab", "energy"), 0, 0), axis=0).reshape(2, 16)
 
 
 def solution(mesh):

time: 135 us -> 134 us (level)
  no operation moved by 1% of the time
where the time goes in v6:
time: 134 us
  Pallas kernels  82.6 us (62%)
  blocking collectives  16.3 us (12%)
  starting transfers between devices  15 us (11%)
  waiting for transfers between devices  11.6 us (9%)
  local copies, waits for them, and re-layouts  4.89 us (4%)
  other arithmetic  1.92 us (1%)
  between operations  1.54 us (1%)
    pallas_call x7, Pallas kernels, call(): pl.pallas_call(kernel, out_shape=outs, in_specs=[SMEM] * len(scalars) + [...  82.6 us
    all_to_all x1, blocking collectives, shards(): lax.all_to_all(sent, ('slab', 'energy'), 0, 0)  16.3 us
    all_to_all x1, waiting for transfers between devices, shards(): lax.all_to_all(jnp.broadcast_to(piece[None], (16, 40, N)), 'energy', 0, 0)  11.6 us
    all_to_all x1, starting transfers between devices, shards(): lax.all_to_all(jnp.broadcast_to(piece[None], (16, 40, N)), 'energy', 0, 0)  8.6 us
    ppermute x1, starting transfers between devices, shards(): after = lax.ppermute(own, 'slab', [(1, 0), (6, 7), (3, 2), (4, 5)])  4.06 us
  transfers between devices with their start and end apart: 4, of which 1 were waited for; matrix products, arithmetic and copies ran while one was open for 0% of the time, Pallas kernels for 33%

profile of v6, /device:TPU:1, one launch (start us, length us, event | category | flops | bytes accessed | tf_op | source)
XLA Modules:
  0.0 133.9 jit_solution(17360053444175894296)
XLA Ops:
  0.0 0.0 copy-start.3
  0.0 0.0 copy-start.2
  0.0 0.8 dynamic_slice.3
  0.8 0.1 iota_compare_fusion
  0.9 0.7 multiply_add_fusion
  1.6 0.1 select_reduce_fusion
  1.7 0.1 pad.8.clone
  1.7 0.8 maximum_maximum_fusion
  2.6 0.9 broadcast_in_dim.56
  3.5 8.6 %all-to-all-start = ((f32[16,40,256]{2,1,0:T(8,128)}), f32[16,40,256]{2,1,0:T(8,128)S(1)}, u32[]{:S(2)}, u32[]{:S(2)}) async-start(f32[16,40,256]{2,1,0:T(8,128)} %broadcast_in_dim.56), calls=%async_computation | async-start | bytes 1310720 | tf_op jit(solution)/shard_map/all_to_all | solution.py:461
  12.1 0.0 copy-done.3
  12.1 0.0 copy-done.2
  12.1 0.1 rev.3
  12.3 11.6 %all-to-all-done.got = f32[16,40,256]{2,1,0:T(8,128)S(1)} async-done(((f32[16,40,256]{2,1,0:T(8,128)}), f32[16,40,256]{2,1,0:T(8,128)S(1)}, u32[]{:S(2)}, u32[]{:S(2)}) %all-to-all-start) | async-done | bytes 655392 | tf_op jit(solution)/shard_map/all_to_all | solution.py:461
  23.8 0.2 shard_map.91.own
  24.1 4.1 %collective-permute-start = (f32[520,256]{1,0:T(8,128)S(1)}, f32[520,256]{1,0:T(8,128)S(1)}, u32[]{:S(2)}, u32[]{:S(2)}) collective-permute-start(f32[520,256]{1,0:T(8,128)S(1)} %shard_map.91.own), channel_id=1, source_target_pairs={{1,0},{6,7},{3,2},{4,5},{9,8},{14,15},{11,10},{12,13},{17,16},{22,... | collective-permute-start | bytes 1597448 | tf_op jit(solution)/shard_map/ppermute | solution.py:468
  28.8 10.8 %shard_map.92 = (f32[1,2,256,256]{3,2,1,0:T(8,128)S(1)}, f32[1,8,256]{2,1,0:T(8,128)S(1)}) custom-call(s32[1]{0:T(128)} %bitcast.flag, s32[1]{0:T(128)} %bitcast.1.inner, f32[1]{0:T(128)S(6)} %copy.18.energy, f32[520,256]{1,0:T(8,128)S(1)} %shard_map.91.own), custom_call_target="tpu_custom_call" | custom-call | flops 134217728 | bytes 262144 | tf_op jit(solution)/shard_map/pallas_call | solution.py:438
  39.6 0.0 collective-permute-done.after
  39.6 10.8 %shard_map.93 = (f32[2,2,256,256]{3,2,1,0:T(8,128)S(1)}, f32[2,8,256]{2,1,0:T(8,128)S(1)}, f32[1304,256]{1,0:T(8,128)S(1)}, f32[520,256]{1,0:T(8,128)S(1)}) custom-call(s32[1]{0:T(128)} %bitcast.flag, s32[1]{0:T(128)} %bitcast.1.inner, f32[1]{0:T(128)S(6)} %copy.18.energy, f32[520,256]{1,0:T(8,128)S(1)} %shard_map.91.own, ...), custom_call_target="tpu_custom_call" | custom-call | flops 134217728 | bytes 262144 | tf_op jit(solution)/shard_map/pallas_call | solution.py:438
  50.4 0.9 collective-permute-start.1
  51.3 21.7 %shard_map.94 = (f32[2,2,256,256]{3,2,1,0:T(8,128)S(1)}, f32[2,8,256]{2,1,0:T(8,128)S(1)}) custom-call(s32[1]{0:T(128)} %bitcast.flag, f32[1]{0:T(128)S(6)} %copy.18.energy, f32[520,256]{1,0:T(8,128)S(1)} %get-tuple-element.21.after, f32[2,2,256,256]{3,2,1,0:T(8,128)S(1)} %get-tuple-element.22.start.m0, f32[2,8,256]{2,1,0:T(8,128)S(1)} %get-tuple-element.23.before.v0), custom_call_target="tpu_custom_call" | custom-call | flops 268435456 | bytes 524288 | tf_op jit(solution)/shard_map/pallas_call | solution.py:438
  73.0 0.0 collective-permute-done.1.mid
  73.0 13.9 %shard_map.95 = (f32[2,256,256]{2,1,0:T(8,128)S(1)}, f32[8,256]{1,0:T(8,128)S(1)}, f32[520,256]{1,0:T(8,128)}) custom-call(s32[1]{0:T(128)} %bitcast.flag, f32[1]{0:T(128)S(6)} %copy.18.energy, f32[2,2,256,256]{3,2,1,0:T(8,128)S(1)} %get-tuple-element.24.start.m1, f32[2,8,256]{2,1,0:T(8,128)S(1)} %get-tuple-element.25.before.v1, ...), custom_call_target="tpu_custom_call" | custom-call | flops 134217728 | bytes 262144 | tf_op jit(solution)/shard_map/pallas_call | solution.py:438
  86.9 0.0 copy-start
  86.9 0.8 copy-done
  87.7 1.5 %collective-permute-start.2 = (f32[520,256]{1,0:T(8,128)}, f32[520,256]{1,0:T(8,128)}, u32[]{:S(2)}, u32[]{:S(2)}) collective-permute-start(f32[520,256]{1,0:T(8,128)} %get-tuple-element.27.ready), channel_id=1, source_target_pairs={{0,7},{7,0},{8,15},{15,8},{16,23},{23,16},{24,31},{31,24},{32,39},... | collective-permute-start | bytes 1597448 | tf_op jit(solution)/shard_map/ppermute | solution.py:499
  89.8 0.0 copy-start.1
  89.8 1.0 copy-done.1
  90.9 11.8 %shard_map.96 = (f32[2,256,256]{2,1,0:T(8,128)S(1)}, f32[8,256]{1,0:T(8,128)S(1)}, f32[2,256,256]{2,1,0:T(8,128)S(1)}) custom-call(f32[520,256]{1,0:T(8,128)} %get-tuple-element.27.ready, f32[2,256,256]{2,1,0:T(8,128)S(1)} %copy-done.1), custom_call_target="tpu_custom_call" | custom-call | flops 134217728 | bytes 262144 | tf_op jit(solution)/shard_map/pallas_call | solution.py:438
  102.6 0.0 collective-permute-done.2.far
  102.6 13.5 %shard_map.97 = f32[8,256]{1,0:T(8,128)S(1)} custom-call(s32[1]{0:T(128)} %bitcast.flag, f32[1]{0:T(128)S(6)} %copy.19.weight, f32[520,256]{1,0:T(8,128)} %collective-permute-done.2.far, f32[2,2,256,256]{3,2,1,0:T(8,128)S(1)} %get-tuple-element.22.start.m0, f32[2,8,256]{2,1,0:T(8,128)S(1)} %get-tuple-element.23.before.v0, ...), custom_call_target="tpu_custom_call" | custom-call | flops 134217728 | bytes 262144 | tf_op jit(solution)/shard_map/pallas_call | solution.py:438
  116.2 0.1 select_n.41
  116.3 0.1 copy.15
  116.4 0.1 select_n.44
  116.5 0.1 copy.16
  116.6 0.1 reshape.40
  116.7 0.1 copy.17
  116.8 16.3 %all_to_all.10 = f32[128,1,32]{2,1,0:T(1,128)S(1)} all-to-all(f32[128,1,32]{2,1,0:T(1,128)S(1)} %copy.17), channel_id=1, replica_groups=mesh['energy'=16,'slab'=8] {'slab','energy'}, dimensions={0} | all-to-all | bytes 32768 | tf_op jit(solution)/shard_map/all_to_all | solution.py:512
  133.1 0.2 reduce_sum.19
  133.3 0.6 reshape.41
  (8 shorter events, 0.1 us)
Async XLA Ops:
  0.0 12.1 %copy-start.3 = (f32[2,1,2,256]{3,2,1,0:T(2,128)S(1)}, f32[2,1,2,256]{3,2,1,0:T(2,128)}, u32[]{:S(2)}) copy-start(f32[2,1,2,256]{3,2,1,0:T(2,128)} %param.17) | copy-start | bytes 12292
  0.0 12.1 %copy-start.2 = (f32[2,256]{1,0:T(2,128)S(1)}, f32[2,256]{1,0:T(2,128)}, u32[]{:S(2)}) copy-start(f32[2,256]{1,0:T(2,128)} %param.14) | copy-start | bytes 6148
  3.5 20.4 %all-to-all-start = ((f32[16,40,256]{2,1,0:T(8,128)}), f32[16,40,256]{2,1,0:T(8,128)S(1)}, u32[]{:S(2)}, u32[]{:S(2)}) async-start(f32[16,40,256]{2,1,0:T(8,128)} %broadcast_in_dim.56), calls=%async_computation | async-start | bytes 1310720 | tf_op jit(solution)/shard_map/all_to_all | solution.py:461
  24.1 15.5 %collective-permute-start = (f32[520,256]{1,0:T(8,128)S(1)}, f32[520,256]{1,0:T(8,128)S(1)}, u32[]{:S(2)}, u32[]{:S(2)}) collective-permute-start(f32[520,256]{1,0:T(8,128)S(1)} %shard_map.91.own), channel_id=1, source_target_pairs={{1,0},{6,7},{3,2},{4,5},{9,8},{14,15},{11,10},{12,13},{17,16},{22,... | collective-permute-start | bytes 1597448 | tf_op jit(solution)/shard_map/ppermute | solution.py:468
  50.4 22.6 %collective-permute-start.1 = (f32[1304,256]{1,0:T(8,128)S(1)}, f32[1304,256]{1,0:T(8,128)S(1)}, u32[]{:S(2)}, u32[]{:S(2)}) collective-permute-start(f32[1304,256]{1,0:T(8,128)S(1)} %get-tuple-element.26), channel_id=1, source_target_pairs={{2,0},{5,7},{10,8},{13,15},{18,16},{21,23},{26,24},{29,31},{34,32}... | collective-permute-start | bytes 4005896 | tf_op jit(solution)/shard_map/ppermute | solution.py:488
  86.9 0.8 copy-start
  87.7 14.9 %collective-permute-start.2 = (f32[520,256]{1,0:T(8,128)}, f32[520,256]{1,0:T(8,128)}, u32[]{:S(2)}, u32[]{:S(2)}) collective-permute-start(f32[520,256]{1,0:T(8,128)} %get-tuple-element.27.ready), channel_id=1, source_target_pairs={{0,7},{7,0},{8,15},{15,8},{16,23},{23,16},{24,31},{31,24},{32,39},... | collective-permute-start | bytes 1597448 | tf_op jit(solution)/shard_map/ppermute | solution.py:499
  89.8 1.0 copy-start.1
